TPU v7x, 128 devices: a whole 4x4x4 slice. The times are simulated.
128 devices in a mesh: dp: 8 (over y, core), tensor: 16 (over x, z).
Axes of the slice: x: 4, y: 4, z: 4, core: 2. Of those that a mesh axis runs over, the one named last changes fastest.
Arguments:
- activations: bfloat16 [8192, 5120], P('dp', 'tensor'), may hold values from -6 to 6
- upstream: bfloat16 [8192, 5120], P('dp', 'tensor'), may hold values from -6 to 6
- gate_pre: bfloat16 [8192, 27648], P('dp', 'tensor'), may hold values from -8 to 8
- up_out: bfloat16 [8192, 27648], P('dp', 'tensor'), may hold values from -6 to 6
- w_down: bfloat16 [27648, 5120], P('tensor'), may hold values from -0.078125 to 0.078125
- proj_in: bfloat16 [64, 5120], P(None, 'tensor'), may hold values from -0.078125 to 0.078125
- proj_out: bfloat16 [64, 27648], P(None, 'tensor'), may hold values from -0.0390625 to 0.0390625
- policy_logp: float32 [32, 256], P('dp', 'tensor'), may hold values from -4 to 0
- ref_logp: float32 [32, 256], P('dp', 'tensor'), may hold values from -4 to 0
- loss_mask: int32 [32, 256], P('dp'), may hold values 0 or 1
- resp_len: int32 [32], P('dp'), may hold values from 32 to 256, as said below
- pair_perm: int32 [8, 4], P('dp'), may hold values from 0 to 3, each once within a row
- chosen_first: int32 [16], P('dp'), may hold values 0 or 1
Outputs:
- pair_grads: float32 [16, 4096], P('dp')
- fisher: float32 [4096, 4096], P('tensor', 'dp')
Inputs may be any that keep to these rules, and one draw needn't show every extreme that they name: `resp_len`: at least 32; every index of dp holds a sequence with the full 256 response tokens.
All inputs are finite; a program needn't handle non-finite values. No bound on the sum of `loss_mask` or of `chosen_first` on one device may be relied on, other than what follows from the above.
Results may differ from a plain program's by a relative error of at most 0.0041.
Values may be sent and summed in bfloat16 or wider, within the bound.
A program may use at most 128 MiB of HBM per device.

v0:
```python
import jax
import jax.numpy as jnp
from jax import lax
from jax.sharding import PartitionSpec as P

BETA = 0.1


def per_device(
    activations,
    upstream,
    gate_pre,
    up_out,
    w_down,
    proj_in,
    proj_out,
    policy_logp,
    ref_logp,
    loss_mask,
    resp_len,
    pair_perm,
    chosen_first,
):
    tokens = upstream.shape[0]
    seqs_here = loss_mask.shape[0]
    length = loss_mask.shape[1]
    rank = proj_in.shape[0]
    tensor_count = lax.axis_size("tensor")
    positions = jnp.arange(length, dtype=jnp.int32)
    live = (positions[None, :] >= (length - resp_len)[:, None]) & (loss_mask == 1)
    weight = live.astype(jnp.float32)
    span = policy_logp.shape[1]
    weight_slice = lax.dynamic_slice_in_dim(weight, lax.axis_index("tensor") * span, span, 1)
    margin = lax.psum(jnp.sum(weight_slice * (policy_logp - ref_logp), axis=1), "tensor")
    hidden_grad = lax.dot_general(
        lax.all_gather(upstream, "tensor", axis=1, tiled=True),
        w_down,
        (((1,), (1,)), ((), ())),
        preferred_element_type=jnp.float32,
    )
    gate = gate_pre.astype(jnp.float32)
    sigma_gate = jax.nn.sigmoid(gate)
    gate_grad = (
        hidden_grad * up_out.astype(jnp.float32) * sigma_gate * (1.0 + gate * (1.0 - sigma_gate))
    ).astype(jnp.bfloat16)
    out_side = jnp.dot(gate_grad, proj_out.T, preferred_element_type=jnp.float32)
    in_side = jnp.dot(activations, proj_in.T, preferred_element_type=jnp.float32)
    token_weight = weight.reshape(tokens, 1)
    out_full, in_full = lax.psum((out_side, in_side), "tensor")
    weighted = (in_full * token_weight).reshape(seqs_here, length, rank)
    blocks = jnp.einsum(
        "sti,stj->sij",
        weighted,
        out_full.reshape(seqs_here, length, rank),
        precision=lax.Precision.HIGHEST,
    )
    blocks = blocks.reshape(seqs_here, rank * rank)
    order = pair_perm[0]
    seq_ids = jnp.arange(seqs_here, dtype=jnp.int32)[None, :]
    pick_first = (order[0::2][:, None] == seq_ids).astype(jnp.float32)
    pick_second = (order[1::2][:, None] == seq_ids).astype(jnp.float32)
    chosen = (chosen_first == 1).astype(jnp.float32)[:, None]
    pick_chosen = chosen * pick_first + (1.0 - chosen) * pick_second
    pick_rejected = chosen * pick_second + (1.0 - chosen) * pick_first
    difference = jnp.dot(pick_chosen - pick_rejected, blocks, precision=lax.Precision.HIGHEST)
    margin_gap = jnp.dot(pick_chosen - pick_rejected, margin, precision=lax.Precision.HIGHEST)
    coeff = -BETA * jax.nn.sigmoid(-BETA * margin_gap)
    pair_grads = coeff[:, None] * difference
    proj_size = rank * rank
    row_count = proj_size // tensor_count
    row_start = lax.axis_index("tensor") * row_count
    mine = lax.dynamic_slice_in_dim(pair_grads, row_start, row_count, 1)
    terms = jnp.dot(mine.T, pair_grads, precision=lax.Precision.HIGHEST)
    fisher = lax.psum_scatter(terms, "dp", scatter_dimension=1, tiled=True)
    return (pair_grads, fisher)


def solution(mesh):
    placed = (
        P("dp", "tensor"),
        P("dp", "tensor"),
        P("dp", "tensor"),
        P("dp", "tensor"),
        P("tensor", None),
        P(None, "tensor"),
        P(None, "tensor"),
        P("dp", "tensor"),
        P("dp", "tensor"),
        P("dp", None),
        P("dp"),
        P("dp", None),
        P("dp"),
    )
    return jax.shard_map(
        per_device,
        mesh=mesh,
        in_specs=placed,
        out_specs=(P("dp", None), P("tensor", "dp")),
        check_vma=False,
    )
```

profile of v0, /device:TPU:1, one launch (start us, length us, event | category | flops | bytes accessed | tf_op | source)
XLA Modules:
  0.0 259.4 jit_solution(12561441562775405897)
XLA Ops:
  7.2 0.0 all-gather.2.cloned.1.call-start
  7.2 0.7 all-gather.2.cloned.1.call-update
  7.9 0.0 all-reduce.3.cloned.1.call-start
  8.0 0.7 broadcast_subtract_fusion
  8.6 0.8 fusion.17
  9.4 0.9 multiply_reduce_fusion
  10.3 0.8 fusion.32
  11.0 1.8 fusion.23
  12.8 81.2 %all-gather.2.cloned.1.call-done = bf16[1024,5120]{0,1:T(8,128)(2,1)} async-done(((bf16[1024,320]{0,1:T(8,128)(2,1)}), bf16[1024,5120]{0,1:T(8,128)(2,1)}) %all-gather.2.cloned.1.call-update) | async-done | bytes 10485776 | tf_op jit(solution)/shard_map/all_gather | solution.py:36
  94.0 30.7 %fusion.6 = f32[1024,64]{0,1:T(8,128)S(1)} fusion(bf16[64,1728]{1,0:T(8,128)(2,1)} %param.19, bf16[1024,1728]{0,1:T(8,128)(2,1)} %param.15, bf16[1024,1728]{0,1:T(8,128)(2,1)} %param.16, bf16[1728,5120]{1,0:T(8,128)(2,1)} %param.17, bf16[1024,5120]{0,1:T(8,128)(2,1)} %all-gather.2.cloned.1.call-done), kind=kOutput, calls=%fused_computation.9 | convolution fusion | flops 18367119360 | bytes 35741696 | tf_op jit(solution)/shard_map/dot_general | solution.py:46
  124.7 0.7 copy.25
  125.4 0.0 all-reduce.3.cloned.1.call-update
  125.4 0.0 reduce-scatter.2.cloned.1.call-start
  125.5 31.4 %psum.21 = f32[4]{0:T(128)S(1)} all-reduce(f32[4]{0:T(128)S(1)} %multiply_reduce_fusion), channel_id=1, replica_groups=mesh['dp'=8,'tensor'=16] {'tensor'}, use_global_device_ids=true, to_apply=%region_1.0 | all-reduce | flops 4 | bytes 32 | tf_op jit(solution)/shard_map/psum | solution.py:34
  156.9 0.1 slice.7
  157.0 0.1 slice.6
  157.1 0.2 fusion.12
  157.3 52.0 %all-reduce.3.cloned.1.call-done = (f32[4,256,64]{1,2,0:T(8,128)}, f32[1024,64]{0,1:T(8,128)}) async-done(((f32[4,256,64]{1,2,0:T(8,128)}, f32[1024,64]{0,1:T(8,128)}), (f32[4,256,64]{1,2,0:T(8,128)}, f32[1024,64]{0,1:T(8,128)})) %all-reduce.3.cloned.1.call-update) | async-done | bytes 524304 | tf_op jit(solution)/shard_map/psum | solution.py:49
  209.3 1.0 broadcast_multiply_fusion
  210.2 1.3 fusion.13
  211.6 0.1 reshape.24
  211.7 0.3 convolution_multiply_fusion
  212.0 5.1 %fusion.18 = f32[256,4096]{1,0:T(8,128)} fusion(f32[2,4096]{1,0:T(2,128)S(1)} %convolution_multiply_fusion, s32[]{:T(128)S(6)} %select_n.7), kind=kOutput, calls=%fused_computation.25 | convolution fusion | flops 25165824 | bytes 4229124 | tf_op jit(solution)/shard_map/dot_general | solution.py:73
  217.2 35.7 %reduce-scatter.2.cloned.1.call-done = f32[256,512]{1,0:T(8,128)} async-done(((f32[256,4096]{1,0:T(8,128)}), f32[256,512]{1,0:T(8,128)}) %reduce-scatter.2.cloned.1.call-update) | async-done | bytes 524304 | tf_op jit(solution)/shard_map/reduce_scatter | solution.py:74
  (12 shorter events, 0.1 us)
Async XLA Ops:
  7.2 3.9 %copy-start = (bf16[1024,320]{0,1:T(8,128)(2,1)S(1)}, bf16[1024,320]{0,1:T(8,128)(2,1)}, u32[]{:S(2)}) copy-start(bf16[1024,320]{0,1:T(8,128)(2,1)} %param.13) | copy-start | bytes 1966084
  7.2 86.8 %all-gather.2.cloned.1.call-start = ((), (), s32[]{:S(2)}) async-start(), calls=%async_computation.1 | async-start | bytes 11141120 | tf_op jit(solution)/shard_map/all_gather | solution.py:36
  7.9 201.3 %all-reduce.3.cloned.1.call-start = ((), (), s32[]{:S(2)}) async-start(), calls=%async_computation.3 | async-start | bytes 1048576 | tf_op jit(solution)/shard_map/psum | solution.py:49
  12.8 112.7 %copy-start.3 = (s32[2]{0:T(128)S(1)}, s32[2]{0:T(128)}, u32[]{:S(2)}) copy-start(s32[2]{0:T(128)} %param.25) | copy-start | bytes 28
  12.8 144.1 %copy-start.2 = (s32[1,4]{1,0:T(1,128)S(1)}, s32[1,4]{1,0:T(1,128)}, u32[]{:S(2)}) copy-start(s32[1,4]{1,0:T(1,128)} %param.24) | copy-start | bytes 52
  125.4 127.4 %reduce-scatter.2.cloned.1.call-start = ((), (), s32[]{:S(2)}) async-start(), calls=%async_computation.2 | async-start | bytes 4718592 | tf_op jit(solution)/shard_map/reduce_scatter | solution.py:74
  212.0 40.8 %copy-start.1 = (f32[2,4096]{1,0:T(2,128)}, f32[2,4096]{1,0:T(2,128)S(1)}, u32[]{:S(2)}) copy-start(f32[2,4096]{1,0:T(2,128)S(1)} %convolution_multiply_fusion) | copy-start | bytes 98308
Sparse Core Ops, SparseCore 0:
  10.2 83.7 all-gather.1
  125.6 83.6 all-reduce.2
  217.3 35.4 reduce-scatter.1
where the time goes:
time: 262 us; the launch traced here: 259 us
  waiting for transfers between devices  170 us (65%)
  matrix products  39.5 us (15%)
  blocking collectives  31.4 us (12%)
  between operations  13.8 us (5%)
  other arithmetic  4.03 us (2%)
    all_gather x1, waiting for transfers between devices, per_device(): lax.all_gather(upstream, 'tensor', axis=1, tiled=True)  81.2 us
    psum x1, waiting for transfers between devices, per_device(): out_full, in_full = lax.psum((out_side, in_side), 'tensor')  52 us
    reduce_scatter x1, waiting for transfers between devices, per_device(): fisher = lax.psum_scatter(terms, 'dp', scatter_dimension=1, tiled=True)  35.7 us
    psum x1, blocking collectives, per_device(): lax.psum(jnp.sum(weight_slice * (policy_logp - ref_logp), axis=1), 'tensor')  31.4 us
    dot_general x1, matrix products, per_device(): jnp.dot(gate_grad, proj_out.T, preferred_element_type=jnp.float32)  30.7 us
  transfers between devices with their start and end apart: 3, of which 3 were waited for; matrix products, arithmetic and copies ran while one was open for 2% of the time, Pallas kernels for 0%

commit v1 on v0

v1 whole, which is shorter than its diff:
```python
import functools

import jax
import jax.numpy as jnp
from jax import lax
from jax.experimental import pallas as pl
from jax.experimental.pallas import tpu as pltpu
from jax.sharding import PartitionSpec as P

BETA = 0.1
F32, BF16, I32 = jnp.float32, jnp.bfloat16, jnp.int32
MESH = pl.DeviceIdType.MESH
NT = (((1,), (1,)), ((), ()))
TN = (((0,), (0,)), ((), ()))

TENSOR = 16
GROUPS = 8
SEQS = 4
LEN = 256
TOKENS = SEQS * LEN
RANK = 64
FEATURES = 320
HIDDEN = 1728
MODEL = TENSOR * FEATURES
CHUNK = 64
ROWS = 160
HALF = 80
PAIR = 2 * CHUNK
ALL_PAIRS = TOKENS // PAIR
PRE = 4


def iota(shape, axis):
    return lax.broadcasted_iota(I32, shape, axis)


def place():
    g, t = lax.axis_index("dp"), lax.axis_index("tensor")
    return g, t, t // 4, t % 4


def stepped(v, by):
    return lax.rem(v + by + 4, 4)


def remote(src, dst, send, recv, g, t):
    return pltpu.make_async_remote_copy(
        src_ref=src, dst_ref=dst, send_sem=send, recv_sem=recv, device_id={"dp": g, "tensor": t}, device_id_type=MESH
    )


def neighbour(axis, by, x, z):
    return stepped(x, by) * 4 + z if axis == 0 else x * 4 + stepped(z, by)


def pair_sign(perm, first, pair, seq):
    side = jnp.where(first[pair] == 1, 1.0, -1.0).astype(F32)
    is_a = jnp.where(perm[0, 2 * pair] == seq, 1.0, 0.0).astype(F32)
    is_b = jnp.where(perm[0, 2 * pair + 1] == seq, 1.0, 0.0).astype(F32)
    return side * (is_a - is_b)


def stage_kernel(
    perm, first, resp, mask, pol, ref, up, act, pin,
    own_o, g1_o, pick_o, sign_o, insum_o, count_o, gap_o,
    pick, cols, own, packed, part, parts, counts, mine,
    keep, ssend, srecv, isend, irecv, csend, crecv,
):
    g, t, x, z = place()
    barrier = pltpu.get_barrier_semaphore()
    for d in range(1, TENSOR):
        pl.semaphore_signal(barrier, inc=1, device_id={"dp": g, "tensor": lax.rem(t + d, TENSOR)}, device_id_type=MESH)
    for d in range(1, GROUPS):
        pl.semaphore_signal(barrier, inc=1, device_id={"dp": lax.rem(g + d, GROUPS), "tensor": t}, device_id_type=MESH)

    row4 = iota((SEQS, LEN), 0)
    start = jnp.zeros((SEQS, LEN), I32)
    for s in range(SEQS):
        start = jnp.where(row4 == s, LEN - resp[s], start)
    live = (iota((SEQS, LEN), 1) >= start) & (mask[...] == 1)
    live_f = jnp.where(live, 1.0, 0.0).astype(F32)
    upto = jnp.where(iota((LEN, LEN), 0) <= iota((LEN, LEN), 1), 1.0, 0.0).astype(BF16)
    running = jnp.dot(live_f.astype(BF16), upto, preferred_element_type=F32)
    begins = [jnp.zeros((1, 1), F32)]
    for s in range(SEQS):
        begins.append(begins[s] + running[s : s + 1, LEN - 1 : LEN])
    for s in range(SEQS):
        at = jnp.where(live[s : s + 1, :], running[s : s + 1, :] - 1.0 + begins[s], -1.0).astype(I32)
        pick[:, s * LEN : (s + 1) * LEN] = jnp.where(iota((TOKENS, LEN), 0) == at, 1.0, 0.0).astype(BF16)
    mine[...] = jnp.broadcast_to(begins[SEQS], (8, 128))

    odd = lax.rem(t, 2)
    r, c = iota((512, FEATURES), 1), iota((512, FEATURES), 0)
    wide = (c < 256) & (r == c + 64 * odd)
    base = jnp.where(odd == 1, 0, 256)
    low = (c >= 256) & (c < 384) & (c - 256 - 64 * odd >= 0) & (c - 256 - 64 * odd < 64) & (r == base + c - 256 - 64 * odd)
    other = 64 * (1 - odd)
    high = (c >= 384) & (c - 384 - other >= 0) & (c - 384 - other < 64) & (r == base + c - 384 - other)
    order = jnp.where(wide | low | high, 1.0, 0.0).astype(BF16)
    cols[...] = jnp.dot(order, up[...], preferred_element_type=F32).astype(BF16)

    def fill(q):
        rows = pl.ds(pl.multiple_of(q * PAIR, PAIR), PAIR)
        moved = lax.dot_general(pick[rows, :], cols[...], NT, preferred_element_type=F32)
        for par in range(2):
            lo = par * CHUNK
            own[par, q, 0:64, :] = moved[lo : lo + 64, 0:128].astype(BF16)
            own[par, q, 64:128, :] = moved[lo : lo + 64, 128:256].astype(BF16)
            own[par, q, 128:160, :] = (moved[lo : lo + 32, 256:384] + moved[lo + 32 : lo + 64, 384:512]).astype(BF16)

    pl.loop(0, PRE)(fill)
    pl.semaphore_wait(barrier, TENSOR - 1 + GROUPS - 1)

    hop1, hop2 = [], []
    for par in range(2):
        slot = x if par == 0 else z
        for k, by in enumerate((1, -1)):
            i = par * 2 + k
            to = neighbour(par, by, x, z)
            hop1.append(remote(own.at[par, 0:PRE], g1_o.at[par, :, slot], ssend.at[i], srecv.at[i], g, to))
            held = g1_o.at[par, :, stepped(slot, -by), k * HALF : (k + 1) * HALF]
            hop2.append(remote(held, held, ssend.at[4 + i], srecv.at[4 + i], g, to))
    for cp in hop1:
        cp.start()
    tells = []
    for d in range(1, GROUPS):
        cp = remote(mine, counts.at[g], csend.at[d - 1], crecv.at[d - 1], lax.rem(g + d, GROUPS), t)
        cp.start()
        tells.append(cp)

    pl.loop(PRE, ALL_PAIRS)(fill)
    keeps = [pltpu.make_async_copy(own, own_o, keep.at[0]), pltpu.make_async_copy(pick, pick_o, keep.at[3])]
    for par in range(2):
        slot = x if par == 0 else z
        keeps.append(pltpu.make_async_copy(own.at[par, 0:PRE], g1_o.at[par, :, slot], keep.at[1 + par]))
    for cp in keeps:
        cp.start()

    packed[...] = lax.dot_general(pick[...], act[...], NT, preferred_element_type=F32).astype(BF16)
    none = jnp.zeros((RANK, FEATURES), BF16)
    sides = lax.dot_general(packed[0:512, :], jnp.concatenate([pin[...], none], 0), NT, preferred_element_type=F32)
    sides += lax.dot_general(packed[512:1024, :], jnp.concatenate([none, pin[...]], 0), NT, preferred_element_type=F32)
    part[...] = sides.reshape(TENSOR, 32, 128)
    halves = []
    for d in range(1, TENSOR):
        to = lax.rem(t + d, TENSOR)
        cp = remote(part.at[to], parts.at[t], isend.at[d - 1], irecv.at[d - 1], g, to)
        cp.start()
        halves.append(cp)

    for cp in hop1:
        cp.wait_recv()
    for cp in hop2:
        cp.start()

    k_at = iota((TOKENS, 128), 0)
    pair_at = lax.rem(iota((TOKENS, 128), 1) // 4, 2)
    sign = jnp.zeros((TOKENS, 128), F32)
    for s in range(SEQS):
        inside = (k_at >= begins[s].astype(I32)) & (k_at < begins[s + 1].astype(I32))
        value = jnp.where(pair_at == 0, pair_sign(perm, first, 0, s), pair_sign(perm, first, 1, s))
        sign = jnp.where(inside, value, sign)
    sign_o[...] = sign.astype(BF16)

    span = jnp.where(iota((LEN, 16), 0) == t * 16 + iota((LEN, 16), 1), 1.0, 0.0).astype(BF16)
    weights = jnp.dot(live_f.astype(BF16), span, preferred_element_type=F32)
    margin = jnp.sum(weights * (pol[...] - ref[...]), axis=1, keepdims=True)
    gaps = []
    for p in range(2):
        gap = jnp.zeros((1, 1), F32)
        for s in range(SEQS):
            gap += pair_sign(perm, first, p, s) * margin[s : s + 1, :]
        gaps.append(gap)
    gap_o[...] = jnp.where(iota((8, 128), 0) < 4, gaps[0], gaps[1])

    for cp in halves:
        cp.wait_recv()
    parts[t] = part[t]
    total = parts[0]
    for i in range(1, TENSOR):
        total += parts[i]
    insum_o[...] = total.astype(BF16)
    for cp in tells:
        cp.wait_recv()
    counts[g] = mine[...]
    most = counts[0]
    for i in range(1, GROUPS):
        most = jnp.maximum(most, counts[i])
    count_o[...] = most.astype(I32)
    for cp in hop2:
        cp.wait_recv()
    for cp in hop1 + hop2 + halves + tells:
        cp.wait_send()
    for cp in keeps:
        cp.wait()


def stage(perm, first, resp, mask, pol, ref, up, act, pin):
    sds = jax.ShapeDtypeStruct
    vmem = pl.BlockSpec(memory_space=pltpu.VMEM)
    smem = pl.BlockSpec(memory_space=pltpu.SMEM)
    hbm = pl.BlockSpec(memory_space=pl.ANY)
    dma = pltpu.SemaphoreType.DMA
    return pl.pallas_call(
        stage_kernel,
        out_shape=(
            sds((2, ALL_PAIRS, ROWS, 128), BF16),
            sds((2, PRE, 4, ROWS, 128), BF16),
            sds((TOKENS, TOKENS), BF16),
            sds((TOKENS, 128), BF16),
            sds((32, 128), BF16),
            sds((8, 128), I32),
            sds((8, 128), F32),
        ),
        in_specs=[smem] * 3 + [vmem] * 6,
        out_specs=(hbm, hbm, hbm, vmem, vmem, vmem, vmem),
        scratch_shapes=[
            pltpu.VMEM((TOKENS, TOKENS), BF16),
            pltpu.VMEM((512, TOKENS), BF16),
            pltpu.VMEM((2, ALL_PAIRS, ROWS, 128), BF16),
            pltpu.VMEM((TOKENS, FEATURES), BF16),
            pltpu.VMEM((TENSOR, 32, 128), F32),
            pltpu.VMEM((TENSOR, 32, 128), F32),
            pltpu.VMEM((GROUPS, 8, 128), F32),
            pltpu.VMEM((8, 128), F32),
            dma((4,)),
            dma((8,)),
            dma((8,)),
            dma((TENSOR - 1,)),
            dma((TENSOR - 1,)),
            dma((GROUPS - 1,)),
            dma((GROUPS - 1,)),
        ],
        compiler_params=pltpu.CompilerParams(collective_id=0, has_side_effects=True, vmem_limit_bytes=56 << 20),
        cost_estimate=pl.CostEstimate(flops=2_000_000_000, bytes_accessed=8_000_000, transcendentals=0),
        name="stage",
    )(perm, first, resp, mask, pol, ref, up, act, pin)


def main_kernel(
    pairs, sign, insum, gap, pout, own_h, g1_h, pick_h, gate_h, upo_h, w_h,
    ends_o,
    blocks, w, gate, upo, pick, m, u, grad, sides, diff, outs, ins, fin, every, rowed, coled,
    load, asend, arecv, fsend, frecv, ssend, srecv, rsend, rrecv, gsend, grecv, psend, precv, csend, crecv,
):
    g, t, x, z = place()
    column_group, column_part = t // 2, lax.rem(t, 2)
    barrier = pltpu.get_barrier_semaphore()
    for d in range(1, TENSOR):
        pl.semaphore_signal(barrier, inc=1, device_id={"dp": g, "tensor": lax.rem(t + d, TENSOR)}, device_id_type=MESH)
    for d in range(1, GROUPS):
        pl.semaphore_signal(barrier, inc=1, device_id={"dp": lax.rem(g + d, GROUPS), "tensor": t}, device_id_type=MESH)
    for d in range(GROUPS):
        for h in range(2):
            of, at = lax.rem(g + d, GROUPS), 2 * g + h

            def greet(of=of, at=at):
                pl.semaphore_signal(barrier, inc=1, device_id={"dp": of, "tensor": at}, device_id_type=MESH)

            if d == 0:
                pl.when(at != t)(greet)
            else:
                greet()

    wide = MODEL // 4
    loads = []
    halves = [
        pltpu.make_async_copy(pick_h.at[0 : pairs * PAIR], pick, load.at[9]),
        pltpu.make_async_copy(gate_h, gate, load.at[0]),
        pltpu.make_async_copy(upo_h, upo, load.at[10]),
    ]
    for par in range(2):
        to = blocks.at[0, 0:PRE, :, z] if par == 0 else blocks.at[1, 0:PRE, x]
        loads.append(pltpu.make_async_copy(g1_h.at[par], to, load.at[1 + par]))
        if pairs > PRE:
            loads.append(pltpu.make_async_copy(own_h.at[par, PRE:pairs], blocks.at[par, PRE:pairs, x, z], load.at[3 + par]))
    w_loads = [pltpu.make_async_copy(w_h.at[:, i * wide : (i + 1) * wide], w.at[:, i * wide : (i + 1) * wide], load.at[5 + i]) for i in range(4)]
    for cp in loads + halves + w_loads:
        cp.start()
    mates = TENSOR - 1 + GROUPS - 1 + TENSOR
    pl.semaphore_wait(barrier, mates - jnp.where(column_group == g, 1, 0))
    for cp in loads:
        cp.wait()

    def second(q, i, hop):
        par, k = i // 2, i % 2
        by = 1 if k == 0 else -1
        if par == 0:
            to = neighbour(1, by, x, z)
            ref = blocks.at[0, q, :, z] if hop == 0 else blocks.at[0, q, :, stepped(z, -by), k * HALF : (k + 1) * HALF]
        else:
            to = neighbour(0, by, x, z)
            ref = blocks.at[1, q, x] if hop == 0 else blocks.at[1, q, stepped(x, -by), :, k * HALF : (k + 1) * HALF]
        return remote(ref, ref, ssend.at[q, hop * 4 + i], srecv.at[q, hop * 4 + i], g, to)

    def ahead(i, hop):
        par, k = i // 2, i % 2
        by = 1 if k == 0 else -1
        to = neighbour(par, by, x, z)
        if hop == 0:
            ref = blocks.at[par, PRE:pairs, x, z]
        elif par == 0:
            ref = blocks.at[0, PRE:pairs, stepped(x, -by), z, k * HALF : (k + 1) * HALF]
        else:
            ref = blocks.at[1, PRE:pairs, x, stepped(z, -by), k * HALF : (k + 1) * HALF]
        return remote(ref, ref, fsend.at[hop * 4 + i], frecv.at[hop * 4 + i], g, to)

    for q in range(2):
        for i in range(4):
            second(q, i, 0).start()
    if pairs > PRE:
        for i in range(4):
            ahead(i, 0).start()
    ins[t] = insum[...]
    gathers = []
    for d in range(1, TENSOR):
        cp = remote(insum, ins.at[t], asend.at[d - 1], arecv.at[d - 1], g, lax.rem(t + d, TENSOR))
        cp.start()
        gathers.append(cp)
    diff[...] = jnp.zeros_like(diff)
    for cp in halves:
        cp.wait()

    def factor(first_pair, count):
        rows = pl.ds(pl.multiple_of(first_pair * PAIR, PAIR), count * PAIR)

        @pl.loop(0, HIDDEN // 432)
        def _(i):
            units = pl.ds(pl.multiple_of(i * 432, 16), 432)
            v = lax.dot_general(gate[units, :], pick[rows, :], NT, preferred_element_type=F32)
            o = lax.dot_general(upo[units, :], pick[rows, :], NT, preferred_element_type=F32)
            sig = jax.nn.sigmoid(v)
            m[units, rows] = o * sig * (1.0 + v * (1.0 - sig))

    def compute(first_pair, count):
        tokens = count * PAIR
        lanes = iota((32, 128), 1) < 64
        for one in range(count):
            q = first_pair + one
            for par in range(2):
                for s in range(TENSOR // 2):
                    a, b = blocks.at[par, q, s // 2, 2 * (s % 2)], blocks.at[par, q, s // 2, 2 * (s % 2) + 1]
                    r, c = one * PAIR + par * CHUNK, s * 640
                    u[r : r + 64, c : c + 128] = a[0:64, :]
                    u[r : r + 64, c + 128 : c + 256] = a[64:128, :]
                    u[r : r + 64, c + 384 : c + 512] = b[0:64, :]
                    u[r : r + 64, c + 512 : c + 640] = b[64:128, :]
                    left, right = a[128:160, :].astype(F32), b[128:160, :].astype(F32)
                    u[r : r + 32, c + 256 : c + 384] = jnp.where(lanes, left, right).astype(BF16)
                    u[r + 32 : r + 64, c + 256 : c + 384] = pltpu.roll(jnp.where(lanes, right, left), 64, 1).astype(BF16)
        rows = pl.ds(pl.multiple_of(first_pair * PAIR, PAIR), tokens)

        @pl.loop(0, HIDDEN // 576)
        def _(i):
            units = pl.ds(pl.multiple_of(i * 576, 16), 576)
            acc = None
            for k in range(4):
                at = slice(k * wide, (k + 1) * wide)
                more = lax.dot_general(w[units, at], u[0:tokens, at], NT, preferred_element_type=F32)
                acc = more if acc is None else acc + more
            grad[units, 0:tokens] = (acc * m[units, rows]).astype(BF16)

        out_side = jnp.dot(pout[...], grad[:, 0:tokens], preferred_element_type=F32)
        r, c = iota((128, 128), 0), iota((128, 128), 1)
        for one in range(count):
            q = first_pair + one
            side_rows = pl.ds(pl.multiple_of(lax.rem(q, 4) * 4, 4), 4)
            spread = jnp.where(r == jnp.where(q >= 4, 64, 0) + (c // 8) * 4 + lax.rem(c, 4), 1.0, 0.0).astype(BF16)
            in_side = jnp.dot(ins[side_rows].reshape(PAIR, 128), spread, preferred_element_type=F32)
            signed = in_side * sign[pl.ds(pl.multiple_of(q * PAIR, PAIR), PAIR), :].astype(F32)
            part = out_side[:, one * PAIR : (one + 1) * PAIR]
            diff[...] += jnp.dot(part, signed, precision=lax.Precision.HIGHEST, preferred_element_type=F32)

    def turn(q):
        for i in range(4):
            second(q, i, 0).wait_recv()
        for i in range(4):
            second(q, i, 1).start()

    def send(q):
        for i in range(4):
            second(q, i, 0).start()

    full, rest = pairs // 2, pairs % 2
    factor(0, 2)

    @pl.loop(0, full + 1)
    def _(n):
        @pl.when(2 * n < pairs)
        def _():
            turn(2 * n)

        if pairs > PRE:

            @pl.when(n == 0)
            def _():
                for i in range(4):
                    ahead(i, 0).wait_recv()
                for i in range(4):
                    ahead(i, 1).start()

            @pl.when(n == 1)
            def _():
                for i in range(4):
                    ahead(i, 1).wait_recv()

        @pl.when(2 * n + 2 < pairs)
        def _():
            send(2 * n + 2)

        @pl.when(n + 1 < full)
        def _():
            factor(2 * n + 2, 2)

        if rest:

            @pl.when(n + 1 == full)
            def _():
                factor(2 * full, 1)

        @pl.when(2 * n + 1 < pairs)
        def _():
            turn(2 * n + 1)

        @pl.when(2 * n + 3 < pairs)
        def _():
            send(2 * n + 3)

        @pl.when(n == 1)
        def _():
            for cp in w_loads:
                cp.wait()
            for cp in gathers:
                cp.wait_recv()

        @pl.when(n >= 1)
        def _():
            for one in range(2):
                for i in range(4):
                    second(2 * n - 2 + one, i, 1).wait_recv()
            compute(2 * n - 2, 2)

    if rest:
        for i in range(4):
            second(pairs - 1, i, 1).wait_recv()
        compute(pairs - 1, 1)

    mine = jnp.concatenate([diff[...].T, jnp.broadcast_to(gap[0:1, 0:1], (128, 64))], 1).reshape(TENSOR, 8, 128)
    upper = (iota((TENSOR, 8, 128), 2) >= 64) & (iota((TENSOR, 8, 128), 1) >= 4)
    outs[...] = jnp.where(upper, gap[4:5, 0:1].reshape(1, 1, 1), mine)
    reduces = []
    for d in range(1, TENSOR):
        to = lax.rem(t + d, TENSOR)
        cp = remote(outs.at[to], sides.at[t], rsend.at[d - 1], rrecv.at[d - 1], g, to)
        cp.start()
        reduces.append(cp)
    sides[t] = outs[t]
    for cp in reduces:
        cp.wait_recv()
    total = jnp.sum(sides[...], axis=0)
    coeff = -BETA * jax.nn.sigmoid(-BETA * total[:, 64:65])
    fin[...] = jnp.where(iota((8, 128), 1) < 64, coeff * total, 0.0)

    ends = []
    for d in range(1, GROUPS):
        ends.append(remote(fin, rowed.at[g], psend.at[d - 1], precv.at[d - 1], lax.rem(g + d, GROUPS), t))
    for d in range(1, TENSOR):
        ends.append(remote(fin, coled.at[g, column_part], csend.at[d], crecv.at[g, column_part], column_group, lax.rem(t + d, TENSOR)))
    for d in range(1, TENSOR):
        ends.append(remote(fin, every.at[t], gsend.at[d - 1], grecv.at[d - 1], g, lax.rem(t + d, TENSOR)))
    for cp in ends:
        cp.start()
    own_column = remote(fin, coled.at[g, column_part], csend.at[0], crecv.at[g, column_part], column_group, t)
    pl.when(column_group != g)(own_column.start)

    @pl.when(column_group == g)
    def _():
        coled[g, column_part] = fin[...]

    rowed[g] = fin[...]
    every[t] = fin[...]

    for d in range(1, GROUPS):
        ends[d - 1].wait_recv()
    for d in range(GROUPS):
        for h in range(2):
            of = lax.rem(g + d, GROUPS)
            cp = remote(fin, coled.at[of, h], csend.at[0], crecv.at[of, h], column_group, t)
            if d == 0:
                pl.when(2 * g + h != t)(cp.wait_recv)
            else:
                cp.wait_recv()

    for cp in ends[-(TENSOR - 1) :]:
        cp.wait_recv()
    ends_o[0:8] = rowed[...]
    ends_o[8:24] = coled[...].reshape(TENSOR, 8, 128)
    ends_o[24:40] = every[...]

    pl.when(column_group != g)(own_column.wait_send)
    for cp in ends + reduces + gathers:
        cp.wait_send()

    @pl.loop(0, pairs)
    def _(q):
        for hop in range(2):
            for i in range(4):
                second(q, i, hop).wait_send()

    if pairs > PRE:
        for hop in range(2):
            for i in range(4):
                ahead(i, hop).wait_send()


def main(pairs, sign, insum, gap, pout, own, g1, pick, gate, upo, w):
    vmem = pl.BlockSpec(memory_space=pltpu.VMEM)
    hbm = pl.BlockSpec(memory_space=pl.ANY)
    dma = pltpu.SemaphoreType.DMA
    return pl.pallas_call(
        functools.partial(main_kernel, pairs),
        out_shape=jax.ShapeDtypeStruct((40, 8, 128), F32),
        in_specs=[vmem] * 4 + [hbm] * 6,
        out_specs=vmem,
        scratch_shapes=[
            pltpu.VMEM((2, pairs, 4, 4, ROWS, 128), BF16),
            pltpu.VMEM((HIDDEN, MODEL), BF16),
            pltpu.VMEM((HIDDEN, TOKENS), BF16),
            pltpu.VMEM((HIDDEN, TOKENS), BF16),
            pltpu.VMEM((pairs * PAIR, TOKENS), BF16),
            pltpu.VMEM((HIDDEN, pairs * PAIR), F32),
            pltpu.VMEM((2 * PAIR, MODEL), BF16),
            pltpu.VMEM((HIDDEN, 2 * PAIR), BF16),
            pltpu.VMEM((TENSOR, 8, 128), F32),
            pltpu.VMEM((RANK, 128), F32),
            pltpu.VMEM((TENSOR, 8, 128), F32),
            pltpu.VMEM((TENSOR, 32, 128), BF16),
            pltpu.VMEM((8, 128), F32),
            pltpu.VMEM((TENSOR, 8, 128), F32),
            pltpu.VMEM((GROUPS, 8, 128), F32),
            pltpu.VMEM((GROUPS, 2, 8, 128), F32),
            dma((11,)),
            dma((TENSOR - 1,)),
            dma((TENSOR - 1,)),
            dma((8,)),
            dma((8,)),
            dma((pairs, 8)),
            dma((pairs, 8)),
            dma((TENSOR - 1,)),
            dma((TENSOR - 1,)),
            dma((TENSOR - 1,)),
            dma((TENSOR - 1,)),
            dma((GROUPS - 1,)),
            dma((GROUPS - 1,)),
            dma((TENSOR,)),
            dma((GROUPS, 2)),
        ],
        compiler_params=pltpu.CompilerParams(collective_id=pairs, has_side_effects=True, vmem_limit_bytes=60 << 20),
        cost_estimate=pl.CostEstimate(flops=3_200_000_000 * pairs, bytes_accessed=30_000_000, transcendentals=8),
        name=f"gather_{pairs}",
    )(sign, insum, gap, pout, own, g1, pick, gate, upo, w)


def final_kernel(ends, grads_o, fisher_o):
    def joined(at, i):
        lanes = iota((GROUPS, 128), 1) < 64
        got = []
        for p in range(2):
            one, two = ends[at, p * 4 + i], ends[at, p * 4 + i + 1]
            got.append(jnp.where(lanes, one, pltpu.roll(two, 64, 1)))
        return got

    columns = [joined(pl.ds(8 + h, GROUPS, 2), i) for h in range(2) for i in (0, 2)]
    rows = [joined(slice(0, GROUPS), i) for i in (0, 2)]
    right = jnp.concatenate([jnp.concatenate(pair, 0) for pair in columns], 1)
    left = jnp.concatenate([jnp.concatenate(pair, 0) for pair in rows], 1)
    fisher_o[...] = lax.dot_general(left, right, TN, precision=lax.Precision.HIGHEST, preferred_element_type=F32)
    lanes = iota((2, 128), 1) < 64
    for c in range(TENSOR):
        tile = ends[24 + c]
        for i in (0, 2):
            one = jnp.concatenate([tile[i : i + 1], tile[4 + i : 5 + i]], 0)
            two = jnp.concatenate([tile[i + 1 : i + 2], tile[5 + i : 6 + i]], 0)
            at = c * 256 + i * 64
            grads_o[:, at : at + 128] = jnp.where(lanes, one, pltpu.roll(two, 64, 1))


def final(ends):
    sds = jax.ShapeDtypeStruct
    vmem = pl.BlockSpec(memory_space=pltpu.VMEM)
    return pl.pallas_call(
        final_kernel,
        out_shape=(sds((2, RANK * RANK), F32), sds((256, 512), F32)),
        in_specs=[vmem],
        out_specs=(vmem, vmem),
        cost_estimate=pl.CostEstimate(flops=4_000_000, bytes_accessed=700_000, transcendentals=0),
        name="final",
    )(ends)


def per_device(
    activations, upstream, gate_pre, up_out, w_down, proj_in, proj_out, policy_logp, ref_logp, loss_mask, resp_len, pair_perm, chosen_first
):
    own, g1, pick, sign, insum, count, gap = stage(
        pair_perm, chosen_first, resp_len, loss_mask, policy_logp, ref_logp, upstream.T, activations.T, proj_in
    )
    args = (sign, insum, gap, proj_out, own, g1, pick, gate_pre.T, up_out.T, w_down)
    if len(SIZES) == 1:
        return final(main(SIZES[0], *args))
    need = (count[0, 0] + PAIR - 1) // PAIR
    index = jnp.zeros((), I32)
    for size in SIZES[:-1]:
        index += jnp.where(need > size, 1, 0)
    return final(lax.switch(index, [functools.partial(main, size) for size in SIZES], *args))


SIZES = (8,)


def solution(mesh):
    placed = (
        P("dp", "tensor"),
        P("dp", "tensor"),
        P("dp", "tensor"),
        P("dp", "tensor"),
        P("tensor", None),
        P(None, "tensor"),
        P(None, "tensor"),
        P("dp", "tensor"),
        P("dp", "tensor"),
        P("dp", None),
        P("dp"),
        P("dp", None),
        P("dp"),
    )
    return jax.shard_map(
        per_device,
        mesh=mesh,
        in_specs=placed,
        out_specs=(P("dp", None), P("tensor", "dp")),
        check_vma=False,
    )
```

time: 262 us -> 108 us (0.41); the launches traced: 259 us -> 108 us
  waiting for transfers between devices: 170 us -> 0 us
  Pallas kernels: 0 us -> 107 us
  matrix products: 39.5 us -> 0 us
  blocking collectives: 31.4 us -> 0 us
  between operations: 13.8 us -> 0.65 us
  other arithmetic: 4.03 us -> 0 us
    pallas_call x0 -> x3, Pallas kernels: none -> 107 us  [the longest x1 83.4 us: main(): pl.pallas_call(functools.partial(main_kernel, pairs), out_shape=jax.Shape...]
    all_gather x1 -> x0, waiting for transfers between devices: 81.2 us -> none  [per_device(): lax.all_gather(upstream, 'tensor', axis=1, tiled=True)]
    psum x1 -> x0, waiting for transfers between devices: 52 us -> none  [per_device(): out_full, in_full = lax.psum((out_side, in_side), 'tensor')]
    dot_general x6 -> x0, matrix products: 39.5 us -> none  [the longest x1 30.7 us: per_device(): jnp.dot(gate_grad, proj_out.T, preferred_element_type=jnp.float32)]
    reduce_scatter x1 -> x0, waiting for transfers between devices: 35.7 us -> none  [per_device(): fisher = lax.psum_scatter(terms, 'dp', scatter_dimension=1, tiled=True)]
    psum x1 -> x0, blocking collectives: 31.4 us -> none  [per_device(): lax.psum(jnp.sum(weight_slice * (policy_logp - ref_logp), axis=1), 'tensor')]
  transfers between devices with their start and end apart: 3 -> 0, of which waited for: 3 -> 0; matrix products, arithmetic and copies ran while one was open for 2% -> 0% of each run, Pallas kernels for 0% -> 0%
where the time goes in v1:
time: 108 us
  Pallas kernels  107 us (99%)
    pallas_call x1, Pallas kernels, main(): pl.pallas_call(functools.partial(main_kernel, pairs), out_shape=jax.Shape...  83.4 us
    pallas_call x1, Pallas kernels, stage(): pl.pallas_call(stage_kernel, out_shape=(sds((2, ALL_PAIRS, ROWS, 128), BF...  21.5 us
    pallas_call x1, Pallas kernels, final(): pl.pallas_call(final_kernel, out_shape=(sds((2, RANK * RANK), F32), sds((...  2.4 us

profile of v1, /device:TPU:1, one launch (start us, length us, event | category | flops | bytes accessed | tf_op | source)
XLA Modules:
  0.0 108.0 jit_solution(1122604634986418297)
XLA Ops:
  0.6 21.5 %stage.1 = (bf16[2,8,160,128]{3,2,1,0:T(8,128)(2,1)}, bf16[2,4,4,160,128]{4,3,2,1,0:T(8,128)(2,1)}, bf16[1024,1024]{1,0:T(8,128)(2,1)}, bf16[1024,128]{1,0:T(8,1...) custom-call(s32[1,4]{1,0:T(1,128)} %perm.1, s32[2]{0:T(128)} %first.1, s32[4]{0:T(128)} %resp.1, ...), custom_call_target="tpu_custom_call" | custom-call | flops 2000000000 | bytes 8000000 | tf_op jit(solution)/shard_map/stage/pallas_call | solution.py:204
  22.1 83.4 %gather_8.1.ends = f32[40,8,128]{2,1,0:T(8,128)} custom-call(bf16[1024,128]{1,0:T(8,128)(2,1)} %get-tuple-element.8.sign, bf16[32,128]{1,0:T(8,128)(2,1)} %get-tuple-element.9.insum, f32[8,128]{1,0:T(8,128)} %get-tuple-element.10.gap, bf16[64,1728]{1,0:T(8,128)(2,1)} %pout.1, bf16[2,8,160,128]{3,2,1,0:T(8,128)(2,1)} %get-tuple-element.11.own_h, ...), custom_call_target="tpu_custom_call" | custom-call | flops 25600000000 | bytes 30000000 | tf_op jit(solution)/shard_map/gather_8/pallas_call | solution.py:520
  105.6 2.4 %final.1 = (f32[2,4096]{1,0:T(2,128)}, f32[256,512]{1,0:T(8,128)}) custom-call(f32[40,8,128]{2,1,0:T(8,128)} %gather_8.1.ends), custom_call_target="tpu_custom_call" | custom-call | flops 4000000 | bytes 700000 | tf_op jit(solution)/shard_map/final/pallas_call | solution.py:591

commit v2 on v1

--- a/solution.py
+++ b/solution.py
@@ -27,6 +27,7 @@
 HALF = 80
 PAIR = 2 * CHUNK
 ALL_PAIRS = TOKENS // PAIR
+SIZES = (4, 5, 6, 7, 8)
 PRE = 4
 
 
@@ -186,7 +187,11 @@
     most = counts[0]
     for i in range(1, GROUPS):
         most = jnp.maximum(most, counts[i])
-    count_o[...] = most.astype(I32)
+    most = jnp.max(most)
+    index = jnp.zeros((), I32)
+    for size in SIZES[:-1]:
+        index += jnp.where(most > size * PAIR, 1, 0)
+    count_o[0] = index
     for cp in hop2:
         cp.wait_recv()
     for cp in hop1 + hop2 + halves + tells:
@@ -209,11 +214,11 @@
             sds((TOKENS, TOKENS), BF16),
             sds((TOKENS, 128), BF16),
             sds((32, 128), BF16),
-            sds((8, 128), I32),
+            sds((1,), I32),
             sds((8, 128), F32),
         ),
         in_specs=[smem] * 3 + [vmem] * 6,
-        out_specs=(hbm, hbm, hbm, vmem, vmem, vmem, vmem),
+        out_specs=(hbm, hbm, hbm, vmem, vmem, smem, vmem),
         scratch_shapes=[
             pltpu.VMEM((TOKENS, TOKENS), BF16),
             pltpu.VMEM((512, TOKENS), BF16),
@@ -607,14 +612,7 @@
     args = (sign, insum, gap, proj_out, own, g1, pick, gate_pre.T, up_out.T, w_down)
     if len(SIZES) == 1:
         return final(main(SIZES[0], *args))
-    need = (count[0, 0] + PAIR - 1) // PAIR
-    index = jnp.zeros((), I32)
-    for size in SIZES[:-1]:
-        index += jnp.where(need > size, 1, 0)
-    return final(lax.switch(index, [functools.partial(main, size) for size in SIZES], *args))
-
-
-SIZES = (8,)
+    return final(lax.switch(count[0], [functools.partial(main, size) for size in SIZES], *args))
 
 
 def solution(mesh):

time: 108 us -> 88.9 us (0.82)
  Pallas kernels: 107 us -> 86.8 us
    pallas_call x1, Pallas kernels: 83.4 us -> 63.7 us  [main(): pl.pallas_call(functools.partial(main_kernel, pairs), out_shape=jax.Shape...]
where the time goes in v2:
time: 88.9 us; the launch traced here: 88.8 us
  Pallas kernels  86.8 us (98%)
  between operations  1.37 us (2%)
    pallas_call x1, Pallas kernels, main(): pl.pallas_call(functools.partial(main_kernel, pairs), out_shape=jax.Shape...  63.7 us
    pallas_call x1, Pallas kernels, stage(): pl.pallas_call(stage_kernel, out_shape=(sds((2, ALL_PAIRS, ROWS, 128), BF...  21.6 us

profile of v2, /device:TPU:1, one launch (start us, length us, event | category | flops | bytes accessed | tf_op | source)
XLA Modules:
  0.0 88.8 jit_solution(11870140061774913833)
XLA Ops:
  0.6 0.0 copy-start
  0.6 0.0 copy-start.1
  0.7 21.6 %stage.1 = (bf16[2,8,160,128]{3,2,1,0:T(8,128)(2,1)}, bf16[2,4,4,160,128]{4,3,2,1,0:T(8,128)(2,1)}, bf16[1024,1024]{1,0:T(8,128)(2,1)}, bf16[1024,128]{1,0:T(8,1...) custom-call(s32[1,4]{1,0:T(1,128)} %perm.1, s32[2]{0:T(128)} %first.1, s32[4]{0:T(128)} %resp.1, ...), custom_call_target="tpu_custom_call" | custom-call | flops 2000000000 | bytes 8000000 | tf_op jit(solution)/shard_map/stage/pallas_call | solution.py:209
  23.0 0.0 copy-done
  23.0 0.0 copy-done.1
  23.0 64.3 %conditional.1 = (f32[40,8,128]{2,1,0:T(8,128)S(1)}) conditional(s32[]{:T(128)} %bitcast.2, (bf16[1024,128]{1,0:T(8,128)(2,1)}, bf16[32,128]{1,0:T(8,128)(2,1)S(1)}, f32[8,128]{1,0:T(8,128)S(1)}, bf16[64,1728]{1,0:T(8,128)(2,1)S(1)}, bf16[2,8,160,128]{3,2,1,0:T(8,128)(2,1)}, ...), branch_computations={%region_0.0_spmd, %region_1.0_spmd, %region_2.0_spmd, %region_3.0_... | conditional | flops 25600000000 | bytes 30000008 | solution.py:615
  23.0 63.7 %gather_5.1 = f32[40,8,128]{2,1,0:T(8,128)S(1)} custom-call(bf16[1024,128]{1,0:T(8,128)(2,1)} %get-tuple-element.116.sign, bf16[32,128]{1,0:T(8,128)(2,1)S(1)} %get-tuple-element.117.insum, f32[8,128]{1,0:T(8,128)S(1)} %get-tuple-element.118.gap, bf16[64,1728]{1,0:T(8,128)(2,1)S(1)} %get-tuple-element.119.pout, ...), custom_call_target="tpu_custom_call" | custom-call | flops 16000000000 | bytes 30000000 | tf_op jit(solution)/shard_map/cond/branch_1_fun/gather_5/pallas_call | solution.py:525
  87.3 1.5 %final.1 = (f32[2,4096]{1,0:T(2,128)}, f32[256,512]{1,0:T(8,128)}) custom-call(f32[40,8,128]{2,1,0:T(8,128)S(1)} %get-tuple-element.172.ends), custom_call_target="tpu_custom_call" | custom-call | flops 4000000 | bytes 700000 | tf_op jit(solution)/shard_map/final/pallas_call | solution.py:596
Async XLA Ops:
  0.6 22.3 %copy-start = (bf16[1024,1728]{0,1:T(8,128)(2,1)S(1)}, bf16[1024,1728]{0,1:T(8,128)(2,1)}, u32[]{:S(2)}) copy-start(bf16[1024,1728]{0,1:T(8,128)(2,1)} %param.20) | copy-start | bytes 10616836
  0.6 22.3 %copy-start.1 = (bf16[64,1728]{1,0:T(8,128)(2,1)S(1)}, bf16[64,1728]{1,0:T(8,128)(2,1)}, u32[]{:S(2)}) copy-start(bf16[64,1728]{1,0:T(8,128)(2,1)} %param.24) | copy-start | bytes 663556

commit v3 on v2

v3 whole, which is shorter than its diff:
```python
import functools

import jax
import jax.numpy as jnp
from jax import lax
from jax.experimental import pallas as pl
from jax.experimental.pallas import tpu as pltpu
from jax.sharding import PartitionSpec as P

BETA = 0.1
F32, BF16, I32 = jnp.float32, jnp.bfloat16, jnp.int32
MESH = pl.DeviceIdType.MESH
NT = (((1,), (1,)), ((), ()))
TN = (((0,), (0,)), ((), ()))

TENSOR = 16
GROUPS = 8
SEQS = 4
LEN = 256
TOKENS = SEQS * LEN
RANK = 64
FEATURES = 320
HIDDEN = 1728
MODEL = TENSOR * FEATURES
CHUNK = 64
WIDE = 2 * CHUNK
ROWS = WIDE + CHUNK // 2
PAIR = 2 * CHUNK
ALL_PAIRS = TOKENS // PAIR
PRE = 512 // PAIR
GROUP = 256 // PAIR
LOOK = 2
SIZES = (4, 5, 6, 7, 8)


def cut(parity):
    return ROWS // 2 if ROWS % 32 == 0 else ROWS // 2 + (8 if parity == 0 else -8)


def iota(shape, axis):
    return lax.broadcasted_iota(I32, shape, axis)


def place():
    g, t = lax.axis_index("dp"), lax.axis_index("tensor")
    return g, t, t // 4, t % 4


def stepped(v, by):
    return lax.rem(v + by + 4, 4)


def remote(src, dst, send, recv, g, t):
    return pltpu.make_async_remote_copy(
        src_ref=src, dst_ref=dst, send_sem=send, recv_sem=recv, device_id={"dp": g, "tensor": t}, device_id_type=MESH
    )


def neighbour(axis, by, x, z):
    return stepped(x, by) * 4 + z if axis == 0 else x * 4 + stepped(z, by)


def greet(g, t):
    barrier = pltpu.get_barrier_semaphore()
    for d in range(1, TENSOR):
        pl.semaphore_signal(barrier, inc=1, device_id={"dp": g, "tensor": lax.rem(t + d, TENSOR)}, device_id_type=MESH)
    for d in range(1, GROUPS):
        pl.semaphore_signal(barrier, inc=1, device_id={"dp": lax.rem(g + d, GROUPS), "tensor": t}, device_id_type=MESH)
    return barrier


def pair_sign(perm, first, pair, seq):
    side = jnp.where(first[pair] == 1, 1.0, -1.0).astype(F32)
    is_a = jnp.where(perm[0, 2 * pair] == seq, 1.0, 0.0).astype(F32)
    is_b = jnp.where(perm[0, 2 * pair + 1] == seq, 1.0, 0.0).astype(F32)
    return side * (is_a - is_b)


def stage_kernel(
    perm, first, resp, mask, pol, ref, up_h, act_h, pin_h,
    own_o, g1_o, pick_o, sign_o, insum_o, count_o, gap_o,
    pick, cols, own, packed, part, parts, counts, mine, up, act, pin,
    load, keep, ssend, srecv, isend, irecv, csend, crecv,
):
    g, t, x, z = place()
    barrier = greet(g, t)
    loads = [pltpu.make_async_copy(*refs, load.at[i]) for i, refs in enumerate(((up_h, up), (act_h, act), (pin_h, pin)))]
    for cp in loads:
        cp.start()

    row4 = iota((SEQS, LEN), 0)
    start = jnp.zeros((SEQS, LEN), I32)
    for s in range(SEQS):
        start = jnp.where(row4 == s, LEN - resp[s], start)
    live = (iota((SEQS, LEN), 1) >= start) & (mask[...] == 1)
    live_f = jnp.where(live, 1.0, 0.0).astype(F32)
    upto = jnp.where(iota((LEN, LEN), 0) <= iota((LEN, LEN), 1), 1.0, 0.0).astype(BF16)
    running = jnp.dot(live_f.astype(BF16), upto, preferred_element_type=F32)
    begins = [jnp.zeros((1, 1), F32)]
    for s in range(SEQS):
        begins.append(begins[s] + running[s : s + 1, LEN - 1 : LEN])

    def choose(half):
        for s in range(SEQS):
            at = jnp.where(live[s : s + 1, :], running[s : s + 1, :] - 1.0 + begins[s], -1.0).astype(I32)
            here = iota((512, LEN), 0) + half * 512 == at
            pick[half * 512 : (half + 1) * 512, s * LEN : (s + 1) * LEN] = jnp.where(here, 1.0, 0.0).astype(BF16)

    choose(0)
    mine[...] = jnp.broadcast_to(begins[SEQS], (8, 128))

    odd = lax.rem(t, 2)
    r, c = iota((512, FEATURES), 1), iota((512, FEATURES), 0)
    wide = (c < 256) & (r == c + 64 * odd)
    base = jnp.where(odd == 1, 0, 256)
    low = (c >= 256) & (c < 384) & (c - 256 - 64 * odd >= 0) & (c - 256 - 64 * odd < 64) & (r == base + c - 256 - 64 * odd)
    other = 64 * (1 - odd)
    high = (c >= 384) & (c - 384 - other >= 0) & (c - 384 - other < 64) & (r == base + c - 384 - other)
    order = jnp.where(wide | low | high, 1.0, 0.0).astype(BF16)
    loads[0].wait()
    cols[...] = jnp.dot(order, up[...], preferred_element_type=F32).astype(BF16)

    def fill(n):
        rows = pl.ds(pl.multiple_of(n * 128, 128), 128)
        moved = lax.dot_general(pick[rows, :], cols[...], NT, preferred_element_type=F32)
        for one in range(128 // PAIR):
            for par in range(2):
                lo, mid, hi = (one * PAIR + par * CHUNK + e for e in (0, CHUNK // 2, CHUNK))
                q = n * (128 // PAIR) + one
                own[par, q, 0:CHUNK, :] = moved[lo:hi, 0:128].astype(BF16)
                own[par, q, CHUNK:WIDE, :] = moved[lo:hi, 128:256].astype(BF16)
                own[par, q, WIDE:ROWS, :] = (moved[lo:mid, 256:384] + moved[mid:hi, 384:512]).astype(BF16)

    hop1, hop2 = [], []
    for half in range(2):
        pairs = slice(half * PRE // 2, (half + 1) * PRE // 2)
        for par in range(2):
            slot = x if par == 0 else z
            for k, by in enumerate((1, -1)):
                i = half * 4 + par * 2 + k
                to = neighbour(par, by, x, z)
                hop1.append(remote(own.at[par, pairs], g1_o.at[par, pairs, slot], ssend.at[i], srecv.at[i], g, to))
                held = g1_o.at[par, pairs, stepped(slot, -by), (0, cut(par))[k] : (cut(par), ROWS)[k]]
                hop2.append(remote(held, held, ssend.at[8 + i], srecv.at[8 + i], g, to))
    pl.loop(0, 2)(fill)
    pl.semaphore_wait(barrier, TENSOR - 1 + GROUPS - 1)
    for cp in hop1[:4]:
        cp.start()
    pl.loop(2, 4)(fill)
    for cp in hop1[4:]:
        cp.start()
    tells = []
    for d in range(1, GROUPS):
        cp = remote(mine, counts.at[g], csend.at[d - 1], crecv.at[d - 1], lax.rem(g + d, GROUPS), t)
        cp.start()
        tells.append(cp)

    choose(1)
    for cp in loads[1:]:
        cp.wait()
    packed[...] = lax.dot_general(pick[...], act[...], NT, preferred_element_type=F32).astype(BF16)
    none = jnp.zeros((RANK, FEATURES), BF16)
    sides = lax.dot_general(packed[0:512, :], jnp.concatenate([pin[...], none], 0), NT, preferred_element_type=F32)
    sides += lax.dot_general(packed[512:1024, :], jnp.concatenate([none, pin[...]], 0), NT, preferred_element_type=F32)
    part[...] = sides.reshape(TENSOR, 32, 128)
    halves = []
    for d in range(1, TENSOR):
        to = lax.rem(t + d, TENSOR)
        cp = remote(part.at[to], parts.at[t], isend.at[d - 1], irecv.at[d - 1], g, to)
        cp.start()
        halves.append(cp)

    for half in range(2):
        for cp in hop1[half * 4 : half * 4 + 4]:
            cp.wait_recv()
        for cp in hop2[half * 4 : half * 4 + 4]:
            cp.start()
    pl.loop(4, 8)(fill)
    keeps = [pltpu.make_async_copy(own, own_o, keep.at[0]), pltpu.make_async_copy(pick, pick_o, keep.at[3])]
    for par in range(2):
        slot = x if par == 0 else z
        keeps.append(pltpu.make_async_copy(own.at[par, 0:PRE], g1_o.at[par, :, slot], keep.at[1 + par]))
    for cp in keeps:
        cp.start()

    k_at = iota((TOKENS, 128), 0)
    pair_at = lax.rem(iota((TOKENS, 128), 1) // 4, 2)
    sign = jnp.zeros((TOKENS, 128), F32)
    for s in range(SEQS):
        inside = (k_at >= begins[s].astype(I32)) & (k_at < begins[s + 1].astype(I32))
        value = jnp.where(pair_at == 0, pair_sign(perm, first, 0, s), pair_sign(perm, first, 1, s))
        sign = jnp.where(inside, value, sign)
    sign_o[...] = sign.astype(BF16)

    span = jnp.where(iota((LEN, 16), 0) == t * 16 + iota((LEN, 16), 1), 1.0, 0.0).astype(BF16)
    weights = jnp.dot(live_f.astype(BF16), span, preferred_element_type=F32)
    margin = jnp.sum(weights * (pol[...] - ref[...]), axis=1, keepdims=True)
    gaps = []
    for p in range(2):
        gap = jnp.zeros((1, 1), F32)
        for s in range(SEQS):
            gap += pair_sign(perm, first, p, s) * margin[s : s + 1, :]
        gaps.append(gap)
    gap_o[...] = jnp.where(iota((8, 128), 0) < 4, gaps[0], gaps[1])

    for cp in halves:
        cp.wait_recv()
    parts[t] = part[t]
    total = parts[0]
    for i in range(1, TENSOR):
        total += parts[i]
    insum_o[...] = total.astype(BF16)
    for cp in tells:
        cp.wait_recv()
    counts[g] = mine[...]
    most = counts[0]
    for i in range(1, GROUPS):
        most = jnp.maximum(most, counts[i])
    most = jnp.max(most)
    index = jnp.zeros((), I32)
    for size in SIZES[:-1]:
        index += jnp.where(most > size * PAIR, 1, 0)
    count_o[0] = index
    for cp in hop2:
        cp.wait_recv()
    for cp in hop1 + hop2 + halves + tells:
        cp.wait_send()
    for cp in keeps:
        cp.wait()


def stage(perm, first, resp, mask, pol, ref, up, act, pin):
    sds = jax.ShapeDtypeStruct
    vmem = pl.BlockSpec(memory_space=pltpu.VMEM)
    smem = pl.BlockSpec(memory_space=pltpu.SMEM)
    hbm = pl.BlockSpec(memory_space=pl.ANY)
    dma = pltpu.SemaphoreType.DMA
    return pl.pallas_call(
        stage_kernel,
        out_shape=(
            sds((2, ALL_PAIRS, ROWS, 128), BF16),
            sds((2, PRE, 4, ROWS, 128), BF16),
            sds((TOKENS, TOKENS), BF16),
            sds((TOKENS, 128), BF16),
            sds((32, 128), BF16),
            sds((1,), I32),
            sds((8, 128), F32),
        ),
        in_specs=[smem] * 3 + [vmem] * 3 + [hbm] * 3,
        out_specs=(hbm, hbm, hbm, vmem, vmem, smem, vmem),
        scratch_shapes=[
            pltpu.VMEM((TOKENS, TOKENS), BF16),
            pltpu.VMEM((512, TOKENS), BF16),
            pltpu.VMEM((2, ALL_PAIRS, ROWS, 128), BF16),
            pltpu.VMEM((TOKENS, FEATURES), BF16),
            pltpu.VMEM((TENSOR, 32, 128), F32),
            pltpu.VMEM((TENSOR, 32, 128), F32),
            pltpu.VMEM((GROUPS, 8, 128), F32),
            pltpu.VMEM((8, 128), F32),
            pltpu.VMEM((FEATURES, TOKENS), BF16),
            pltpu.VMEM((FEATURES, TOKENS), BF16),
            pltpu.VMEM((RANK, FEATURES), BF16),
            dma((3,)),
            dma((4,)),
            dma((16,)),
            dma((16,)),
            dma((TENSOR - 1,)),
            dma((TENSOR - 1,)),
            dma((GROUPS - 1,)),
            dma((GROUPS - 1,)),
        ],
        compiler_params=pltpu.CompilerParams(collective_id=0, has_side_effects=True, vmem_limit_bytes=56 << 20),
        cost_estimate=pl.CostEstimate(flops=2_000_000_000, bytes_accessed=8_000_000, transcendentals=0),
        name="stage",
    )(perm, first, resp, mask, pol, ref, up, act, pin)


def main_kernel(
    pairs, gap, insum_h, sign_h, pout_h, own_h, g1_h, pick_h, gate_h, upo_h, w_h,
    ends_o,
    blocks, w, gate, upo, pick, sign, pout, m, u, grad, sides, diff, outs, ins, fin, every, rowed, coled,
    load, asend, arecv, fsend, frecv, ssend, srecv, rsend, rrecv, gsend, grecv, psend, precv, csend, crecv,
):
    g, t, x, z = place()
    column_group, column_part = t // 2, lax.rem(t, 2)
    skip = pairs % GROUP
    total = skip + pairs
    early = skip + PRE
    groups = total // GROUP
    barrier = greet(g, t)
    for d in range(GROUPS):
        for h in range(2):
            of, at = lax.rem(g + d, GROUPS), 2 * g + h

            def tell(of=of, at=at):
                pl.semaphore_signal(barrier, inc=1, device_id={"dp": of, "tensor": at}, device_id_type=MESH)

            if d == 0:
                pl.when(at != t)(tell)
            else:
                tell()

    wide = MODEL // 4
    first_loads = []
    for par in range(2):
        to = blocks.at[0, skip:early, :, z] if par == 0 else blocks.at[1, skip:early, x]
        first_loads.append(pltpu.make_async_copy(g1_h.at[par], to, load.at[par]))
        if pairs > PRE:
            first_loads.append(pltpu.make_async_copy(own_h.at[par, PRE:pairs], blocks.at[par, early:total, x, z], load.at[2 + par]))
    first_loads.append(pltpu.make_async_copy(insum_h, ins.at[t], load.at[4]))
    factor_loads = [
        pltpu.make_async_copy(pick_h.at[0 : pairs * PAIR], pick.at[skip * PAIR : total * PAIR], load.at[5]),
        pltpu.make_async_copy(gate_h, gate, load.at[6]),
        pltpu.make_async_copy(upo_h, upo, load.at[7]),
    ]
    last_loads = [pltpu.make_async_copy(sign_h.at[0 : pairs * PAIR], sign.at[skip * PAIR : total * PAIR], load.at[8]), pltpu.make_async_copy(pout_h, pout, load.at[9])]
    for i in range(4):
        at = slice(i * wide, (i + 1) * wide)
        last_loads.append(pltpu.make_async_copy(w_h.at[:, at], w.at[:, at], load.at[10 + i]))
    for cp in first_loads + factor_loads + last_loads:
        cp.start()
    mates = TENSOR - 1 + GROUPS - 1 + TENSOR
    pl.semaphore_wait(barrier, mates - jnp.where(column_group == g, 1, 0))
    for cp in first_loads:
        cp.wait()

    def part_of(k, parity):
        return slice(0, cut(parity)) if k == 0 else slice(cut(parity), ROWS)

    def second(q, i, hop, parity=0):
        par, k = i // 2, i % 2
        by = 1 if k == 0 else -1
        if par == 0:
            to = neighbour(1, by, x, z)
            ref = blocks.at[0, q, :, z] if hop == 0 else blocks.at[0, q, :, stepped(z, -by), part_of(k, parity)]
        else:
            to = neighbour(0, by, x, z)
            ref = blocks.at[1, q, x] if hop == 0 else blocks.at[1, q, stepped(x, -by), :, part_of(k, parity)]
        return remote(ref, ref, ssend.at[q, hop * 4 + i], srecv.at[q, hop * 4 + i], g, to)

    def ahead(i, hop):
        par, k = i // 2, i % 2
        by = 1 if k == 0 else -1
        to = neighbour(par, by, x, z)
        if hop == 0:
            ref = blocks.at[par, early:total, x, z]
        elif par == 0:
            ref = blocks.at[0, early:total, stepped(x, -by), z, part_of(k, 0)]
        else:
            ref = blocks.at[1, early:total, x, stepped(z, -by), part_of(k, 1)]
        return remote(ref, ref, fsend.at[hop * 4 + i], frecv.at[hop * 4 + i], g, to)

    def send(q):
        for i in range(4):
            second(q, i, 0).start()

    def turn(q, parity):
        for i in range(4):
            second(q, i, 0).wait_recv()
        for i in range(4):
            second(q, i, 1, parity).start()

    def arrive(q, parity):
        for i in range(4):
            second(q, i, 1, parity).wait_recv()

    if pairs > PRE:
        for i in range(4):
            ahead(i, 0).start()
    send(skip)
    gathers = []
    for d in range(1, TENSOR):
        cp = remote(ins.at[t], ins.at[t], asend.at[d - 1], arecv.at[d - 1], g, lax.rem(t + d, TENSOR))
        cp.start()
        gathers.append(cp)
    for q in range(skip + 1, skip + LOOK):
        send(q)
    diff[...] = jnp.zeros_like(diff)
    if skip:
        pick[0:PAIR, :] = jnp.zeros((PAIR, TOKENS), BF16)
        sign[0:PAIR, :] = jnp.zeros((PAIR, 128), BF16)
        u[0:PAIR, :] = jnp.zeros((PAIR, MODEL), BF16)

    def tokens_of(n, count):
        return pl.ds(pl.multiple_of(n * GROUP * PAIR, PAIR), count * PAIR)

    def factor(n, count):
        rows = tokens_of(n, count)

        @pl.loop(0, HIDDEN // 432)
        def _(i):
            units = pl.ds(pl.multiple_of(i * 432, 16), 432)
            v = lax.dot_general(gate[units, :], pick[rows, :], NT, preferred_element_type=F32)
            o = lax.dot_general(upo[units, :], pick[rows, :], NT, preferred_element_type=F32)
            sig = jax.nn.sigmoid(v)
            m[units, rows] = o * sig * (1.0 + v * (1.0 - sig))

    def assemble(q, one):
        lanes = iota((CHUNK // 2, 128), 1) < 64
        for par in range(2):
            for s in range(TENSOR // 2):
                a, b = blocks.at[par, q, s // 2, 2 * (s % 2)], blocks.at[par, q, s // 2, 2 * (s % 2) + 1]
                c, base = s * 640, one * PAIR + par * CHUNK
                whole = pl.ds(pl.multiple_of(base, CHUNK), CHUNK)
                u[whole, c : c + 128] = a[0:CHUNK, :]
                u[whole, c + 128 : c + 256] = a[CHUNK:WIDE, :]
                u[whole, c + 384 : c + 512] = b[0:CHUNK, :]
                u[whole, c + 512 : c + 640] = b[CHUNK:WIDE, :]
                left, right = a[WIDE:ROWS, :].astype(F32), b[WIDE:ROWS, :].astype(F32)
                half = CHUNK // 2
                front, back = pl.ds(pl.multiple_of(base, half), half), pl.ds(pl.multiple_of(base + half, half), half)
                u[front, c + 256 : c + 384] = jnp.where(lanes, left, right).astype(BF16)
                u[back, c + 256 : c + 384] = pltpu.roll(jnp.where(lanes, right, left), 64, 1).astype(BF16)

    def multiply(n, count, i):
        units = pl.ds(pl.multiple_of(i * 576, 16), 576)
        acc = None
        for k in range(4):
            at = slice(k * wide, (k + 1) * wide)
            more = lax.dot_general(w[units, at], u[0 : count * PAIR, at], NT, preferred_element_type=F32)
            acc = more if acc is None else acc + more
        grad[units, 0 : count * PAIR] = (acc * m[units, tokens_of(n, count)]).astype(BF16)

    def project(n, count):
        out_side = jnp.dot(pout[...], grad[:, 0 : count * PAIR], preferred_element_type=F32)
        high = out_side.astype(BF16)
        low = (out_side - high.astype(F32)).astype(BF16)
        both = jnp.dot(jnp.concatenate([high, low], 0), sign[tokens_of(n, count), :], preferred_element_type=F32)
        diff[...] += both[0:RANK] + both[RANK:]

    def sign_sides():
        r, c = iota((128, 128), 0), iota((128, 128), 1)

        @pl.loop(0, pairs * PAIR // 64)
        def _(n):
            at = pl.ds(pl.multiple_of(lax.rem(n, 8) * 2, 2), 2)
            spread = jnp.where(r == jnp.where(n >= 8, 64, 0) + (c // 8) * 4 + lax.rem(c, 4), 1.0, 0.0).astype(BF16)
            in_side = jnp.dot(ins[at].reshape(64, 128), spread, preferred_element_type=F32)
            rows = pl.ds(pl.multiple_of(skip * PAIR + n * 64, 64), 64)
            sign[rows, :] = (in_side * sign[rows, :].astype(F32)).astype(BF16)

    for cp in factor_loads:
        cp.wait()
    factor(0, GROUP)

    def gather_in(n):
        for e in range(GROUP):
            pl.when(n * GROUP + e >= skip)(lambda e=e: arrive(n * GROUP + e, e))

        @pl.loop(0, GROUP)
        def _(e):
            pl.when(n * GROUP + e >= skip)(lambda: assemble(n * GROUP + e, e))

    def pass_on(q, parity):
        pl.when((q >= skip) & (q < total))(lambda: turn(q, parity))
        if pairs > PRE and parity == skip:

            @pl.when(q == skip)
            def _():
                for i in range(4):
                    ahead(i, 0).wait_recv()
                for i in range(4):
                    ahead(i, 1).start()

            @pl.when(q + LOOK == early)
            def _():
                for i in range(4):
                    ahead(i, 1).wait_recv()

        pl.when((q >= skip) & (q + LOOK < total))(lambda: send(q + LOOK))

    @pl.loop(0, groups + 1)
    def _(n):
        pass_on(n * GROUP, 0)
        pl.when(n >= 1)(lambda: gather_in(n - 1))

        @pl.loop(0, 3)
        def _(i):
            pl.when(n >= 1)(lambda: multiply(n - 1, GROUP, i))

            @pl.when(i == 0)
            def _():
                if skip:
                    pass_on(n * GROUP + 1, 1)
                pl.when(n == 0)(lambda: factor(1, GROUP))
                if not skip:
                    pass_on(n * GROUP + 1, 1)

        pl.when(n >= 1)(lambda: project(n - 1, GROUP))

        @pl.when(n == 0)
        def _():
            for cp in gathers:
                cp.wait_recv()
            for cp in last_loads:
                cp.wait()
            sign_sides()

        pl.when(n + 2 < groups)(lambda: factor(n + 2, GROUP))

    mine = jnp.concatenate([diff[...].T, jnp.broadcast_to(gap[0:1, 0:1], (128, 64))], 1).reshape(TENSOR, 8, 128)
    upper = (iota((TENSOR, 8, 128), 2) >= 64) & (iota((TENSOR, 8, 128), 1) >= 4)
    outs[...] = jnp.where(upper, gap[4:5, 0:1].reshape(1, 1, 1), mine)
    reduces = []
    for d in range(1, TENSOR):
        to = lax.rem(t + d, TENSOR)
        cp = remote(outs.at[to], sides.at[t], rsend.at[d - 1], rrecv.at[d - 1], g, to)
        cp.start()
        reduces.append(cp)
    sides[t] = outs[t]
    for cp in reduces:
        cp.wait_recv()
    summed = jnp.sum(sides[...], axis=0)
    coeff = -BETA * jax.nn.sigmoid(-BETA * summed[:, 64:65])
    fin[...] = jnp.where(iota((8, 128), 1) < 64, coeff * summed, 0.0)

    ends = []
    for d in range(1, GROUPS):
        ends.append(remote(fin, rowed.at[g], psend.at[d - 1], precv.at[d - 1], lax.rem(g + d, GROUPS), t))
    for d in range(1, TENSOR):
        ends.append(remote(fin, coled.at[g, column_part], csend.at[d], crecv.at[g, column_part], column_group, lax.rem(t + d, TENSOR)))
    for d in range(1, TENSOR):
        ends.append(remote(fin, every.at[t], gsend.at[d - 1], grecv.at[d - 1], g, lax.rem(t + d, TENSOR)))
    for cp in ends:
        cp.start()
    own_column = remote(fin, coled.at[g, column_part], csend.at[0], crecv.at[g, column_part], column_group, t)
    pl.when(column_group != g)(own_column.start)

    @pl.when(column_group == g)
    def _():
        coled[g, column_part] = fin[...]

    rowed[g] = fin[...]
    every[t] = fin[...]

    for d in range(1, GROUPS):
        ends[d - 1].wait_recv()
    for d in range(GROUPS):
        for h in range(2):
            of = lax.rem(g + d, GROUPS)
            cp = remote(fin, coled.at[of, h], csend.at[0], crecv.at[of, h], column_group, t)
            if d == 0:
                pl.when(2 * g + h != t)(cp.wait_recv)
            else:
                cp.wait_recv()

    for cp in ends[-(TENSOR - 1) :]:
        cp.wait_recv()
    ends_o[0:8] = rowed[...]
    ends_o[8:24] = coled[...].reshape(TENSOR, 8, 128)
    ends_o[24:40] = every[...]

    pl.when(column_group != g)(own_column.wait_send)
    for cp in ends + reduces + gathers:
        cp.wait_send()

    @pl.loop(skip, total)
    def _(q):
        for i in range(4):
            second(q, i, 0).wait_send()

    for q in range(skip, total):
        for i in range(4):
            second(q, i, 1, q % 2).wait_send()

    if pairs > PRE:
        for hop in range(2):
            for i in range(4):
                ahead(i, hop).wait_send()


def main(pairs, gap, insum, sign, pout, own, g1, pick, gate, upo, w):
    total = pairs + pairs % GROUP
    vmem = pl.BlockSpec(memory_space=pltpu.VMEM)
    hbm = pl.BlockSpec(memory_space=pl.ANY)
    dma = pltpu.SemaphoreType.DMA
    return pl.pallas_call(
        functools.partial(main_kernel, pairs),
        out_shape=jax.ShapeDtypeStruct((40, 8, 128), F32),
        in_specs=[vmem] + [hbm] * 9,
        out_specs=vmem,
        scratch_shapes=[
            pltpu.VMEM((2, total, 4, 4, ROWS, 128), BF16),
            pltpu.VMEM((HIDDEN, MODEL), BF16),
            pltpu.VMEM((HIDDEN, TOKENS), BF16),
            pltpu.VMEM((HIDDEN, TOKENS), BF16),
            pltpu.VMEM((total * PAIR, TOKENS), BF16),
            pltpu.VMEM((total * PAIR, 128), BF16),
            pltpu.VMEM((RANK, HIDDEN), BF16),
            pltpu.VMEM((HIDDEN, total * PAIR), F32),
            pltpu.VMEM((GROUP * PAIR, MODEL), BF16),
            pltpu.VMEM((HIDDEN, GROUP * PAIR), BF16),
            pltpu.VMEM((TENSOR, 8, 128), F32),
            pltpu.VMEM((RANK, 128), F32),
            pltpu.VMEM((TENSOR, 8, 128), F32),
            pltpu.VMEM((TENSOR, 32, 128), BF16),
            pltpu.VMEM((8, 128), F32),
            pltpu.VMEM((TENSOR, 8, 128), F32),
            pltpu.VMEM((GROUPS, 8, 128), F32),
            pltpu.VMEM((GROUPS, 2, 8, 128), F32),
            dma((14,)),
            dma((TENSOR - 1,)),
            dma((TENSOR - 1,)),
            dma((8,)),
            dma((8,)),
            dma((total, 8)),
            dma((total, 8)),
            dma((TENSOR - 1,)),
            dma((TENSOR - 1,)),
            dma((TENSOR - 1,)),
            dma((TENSOR - 1,)),
            dma((GROUPS - 1,)),
            dma((GROUPS - 1,)),
            dma((TENSOR,)),
            dma((GROUPS, 2)),
        ],
        compiler_params=pltpu.CompilerParams(collective_id=pairs, has_side_effects=True, vmem_limit_bytes=60 << 20),
        cost_estimate=pl.CostEstimate(flops=25_000_000 * PAIR * pairs, bytes_accessed=30_000_000, transcendentals=8),
        name=f"gather_{pairs}",
    )(gap, insum, sign, pout, own, g1, pick, gate, upo, w)


def final_kernel(ends, grads_o, fisher_o):
    def joined(at, i):
        lanes = iota((GROUPS, 128), 1) < 64
        got = []
        for p in range(2):
            one, two = ends[at, p * 4 + i], ends[at, p * 4 + i + 1]
            got.append(jnp.where(lanes, one, pltpu.roll(two, 64, 1)))
        return got

    columns = [joined(pl.ds(8 + h, GROUPS, 2), i) for h in range(2) for i in (0, 2)]
    rows = [joined(slice(0, GROUPS), i) for i in (0, 2)]
    right = jnp.concatenate([jnp.concatenate(pair, 0) for pair in columns], 1)
    left = jnp.concatenate([jnp.concatenate(pair, 0) for pair in rows], 1)
    fisher_o[...] = lax.dot_general(left, right, TN, precision=lax.Precision.HIGHEST, preferred_element_type=F32)
    lanes = iota((2, 128), 1) < 64
    for c in range(TENSOR):
        tile = ends[24 + c]
        for i in (0, 2):
            one = jnp.concatenate([tile[i : i + 1], tile[4 + i : 5 + i]], 0)
            two = jnp.concatenate([tile[i + 1 : i + 2], tile[5 + i : 6 + i]], 0)
            at = c * 256 + i * 64
            grads_o[:, at : at + 128] = jnp.where(lanes, one, pltpu.roll(two, 64, 1))


def final(ends):
    sds = jax.ShapeDtypeStruct
    vmem = pl.BlockSpec(memory_space=pltpu.VMEM)
    return pl.pallas_call(
        final_kernel,
        out_shape=(sds((2, RANK * RANK), F32), sds((256, 512), F32)),
        in_specs=[vmem],
        out_specs=(vmem, vmem),
        cost_estimate=pl.CostEstimate(flops=4_000_000, bytes_accessed=700_000, transcendentals=0),
        name="final",
    )(ends)


def per_device(
    activations, upstream, gate_pre, up_out, w_down, proj_in, proj_out, policy_logp, ref_logp, loss_mask, resp_len, pair_perm, chosen_first
):
    own, g1, pick, sign, insum, count, gap = stage(
        pair_perm, chosen_first, resp_len, loss_mask, policy_logp, ref_logp, upstream.T, activations.T, proj_in
    )
    args = (gap, insum, sign, proj_out, own, g1, pick, gate_pre.T, up_out.T, w_down)
    if len(SIZES) == 1:
        return final(main(SIZES[0], *args))
    return final(lax.switch(count[0], [functools.partial(main, size) for size in SIZES], *args))


def solution(mesh):
    placed = (
        P("dp", "tensor"),
        P("dp", "tensor"),
        P("dp", "tensor"),
        P("dp", "tensor"),
        P("tensor", None),
        P(None, "tensor"),
        P(None, "tensor"),
        P("dp", "tensor"),
        P("dp", "tensor"),
        P("dp", None),
        P("dp"),
        P("dp", None),
        P("dp"),
    )
    return jax.shard_map(
        per_device,
        mesh=mesh,
        in_specs=placed,
        out_specs=(P("dp", None), P("tensor", "dp")),
        check_vma=False,
    )
```

time: 88.9 us -> 83.2 us (0.936)
  Pallas kernels: 86.8 us -> 81.1 us
    pallas_call x1, Pallas kernels: 63.7 us -> 58.4 us  [main(): pl.pallas_call(functools.partial(main_kernel, pairs), out_shape=jax.Shape...]
where the time goes in v3:
time: 83.2 us; the launch traced here: 83 us
  Pallas kernels  81.1 us (97%)
  between operations  1.37 us (2%)
    pallas_call x1, Pallas kernels, main(): pl.pallas_call(functools.partial(main_kernel, pairs), out_shape=jax.Shape...  58.4 us
    pallas_call x1, Pallas kernels, stage(): pl.pallas_call(stage_kernel, out_shape=(sds((2, ALL_PAIRS, ROWS, 128), BF...  21.2 us

profile of v3, /device:TPU:1, one launch (start us, length us, event | category | flops | bytes accessed | tf_op | source)
XLA Modules:
  0.0 83.0 jit_solution(5469726701509869817)
XLA Ops:
  0.6 0.0 copy-start
  0.6 0.0 copy-start.1
  0.7 21.2 %stage.1 = (bf16[2,8,160,128]{3,2,1,0:T(8,128)(2,1)}, bf16[2,4,4,160,128]{4,3,2,1,0:T(8,128)(2,1)}, bf16[1024,1024]{1,0:T(8,128)(2,1)}, bf16[1024,128]{1,0:T(8,1...) custom-call(s32[1,4]{1,0:T(1,128)} %perm.1, s32[2]{0:T(128)} %first.1, s32[4]{0:T(128)} %resp.1, ...), custom_call_target="tpu_custom_call" | custom-call | flops 2000000000 | bytes 8000000 | tf_op jit(solution)/shard_map/stage/pallas_call | solution.py:238
  22.6 0.0 copy-done
  22.6 0.0 copy-done.1
  22.6 59.0 %conditional.1 = (f32[40,8,128]{2,1,0:T(8,128)S(1)}) conditional(s32[]{:T(128)} %bitcast.2, (f32[8,128]{1,0:T(8,128)S(1)}, bf16[32,128]{1,0:T(8,128)(2,1)S(1)}, bf16[1024,128]{1,0:T(8,128)(2,1)}, bf16[64,1728]{1,0:T(8,128)(2,1)S(1)}, bf16[2,8,160,128]{3,2,1,0:T(8,128)(2,1)}, ...), branch_computations={%region_0.0_spmd, %region_1.0_spmd, %region_2.0_spmd, %region_3.0_... | conditional | flops 25600000000 | bytes 30000008 | solution.py:669
  22.6 58.4 %gather_5.1 = f32[40,8,128]{2,1,0:T(8,128)S(1)} custom-call(f32[8,128]{1,0:T(8,128)S(1)} %get-tuple-element.116.gap, bf16[32,128]{1,0:T(8,128)(2,1)S(1)} %get-tuple-element.117.insum_h, bf16[1024,128]{1,0:T(8,128)(2,1)} %get-tuple-element.118.sign_h, bf16[64,1728]{1,0:T(8,128)(2,1)S(1)} %get-tuple-element.119.pout_h, ...), custom_call_target="tpu_custom_call" | custom-call | flops 16000000000 | bytes 30000000 | tf_op jit(solution)/shard_map/cond/branch_1_fun/gather_5/pallas_call | solution.py:577
  81.6 1.5 %final.1 = (f32[2,4096]{1,0:T(2,128)}, f32[256,512]{1,0:T(8,128)}) custom-call(f32[40,8,128]{2,1,0:T(8,128)S(1)} %get-tuple-element.172.ends), custom_call_target="tpu_custom_call" | custom-call | flops 4000000 | bytes 700000 | tf_op jit(solution)/shard_map/final/pallas_call | solution.py:650
Async XLA Ops:
  0.6 21.9 %copy-start = (bf16[1024,1728]{0,1:T(8,128)(2,1)S(1)}, bf16[1024,1728]{0,1:T(8,128)(2,1)}, u32[]{:S(2)}) copy-start(bf16[1024,1728]{0,1:T(8,128)(2,1)} %param.20) | copy-start | bytes 10616836
  0.6 21.9 %copy-start.1 = (bf16[64,1728]{1,0:T(8,128)(2,1)S(1)}, bf16[64,1728]{1,0:T(8,128)(2,1)}, u32[]{:S(2)}) copy-start(bf16[64,1728]{1,0:T(8,128)(2,1)} %param.24) | copy-start | bytes 663556

commit v4 on v3

--- a/solution.py
+++ b/solution.py
@@ -33,6 +33,9 @@
 SIZES = (4, 5, 6, 7, 8)
 
 
+FAR = (10, 6, 14, 9, 11, 2, 8, 5, 7, 13, 15, 1, 3, 4, 12)
+
+
 def cut(parity):
     return ROWS // 2 if ROWS % 32 == 0 else ROWS // 2 + (8 if parity == 0 else -8)
 
@@ -62,7 +65,7 @@
 
 def greet(g, t):
     barrier = pltpu.get_barrier_semaphore()
-    for d in range(1, TENSOR):
+    for d in FAR:
         pl.semaphore_signal(barrier, inc=1, device_id={"dp": g, "tensor": lax.rem(t + d, TENSOR)}, device_id_type=MESH)
     for d in range(1, GROUPS):
         pl.semaphore_signal(barrier, inc=1, device_id={"dp": lax.rem(g + d, GROUPS), "tensor": t}, device_id_type=MESH)
@@ -77,16 +80,18 @@
 
 
 def stage_kernel(
-    perm, first, resp, mask, pol, ref, up_h, act_h, pin_h,
+    perm, first, resp, mask_h, pol_h, ref_h, up_h, act_h, pin_h,
     own_o, g1_o, pick_o, sign_o, insum_o, count_o, gap_o,
-    pick, cols, own, packed, part, parts, counts, mine, up, act, pin,
+    pick, cols, own, packed, part, parts, counts, mine, up, act, pin, mask, pol, ref,
     load, keep, ssend, srecv, isend, irecv, csend, crecv,
 ):
     g, t, x, z = place()
+    pieces = ((mask_h, mask), (up_h, up), (act_h, act), (pin_h, pin), (pol_h, pol), (ref_h, ref))
+    loads = [pltpu.make_async_copy(*refs, load.at[i]) for i, refs in enumerate(pieces)]
+    for cp in loads:
+        cp.start()
     barrier = greet(g, t)
-    loads = [pltpu.make_async_copy(*refs, load.at[i]) for i, refs in enumerate(((up_h, up), (act_h, act), (pin_h, pin)))]
-    for cp in loads:
-        cp.start()
+    loads[0].wait()
 
     row4 = iota((SEQS, LEN), 0)
     start = jnp.zeros((SEQS, LEN), I32)
@@ -117,7 +122,7 @@
     other = 64 * (1 - odd)
     high = (c >= 384) & (c - 384 - other >= 0) & (c - 384 - other < 64) & (r == base + c - 384 - other)
     order = jnp.where(wide | low | high, 1.0, 0.0).astype(BF16)
-    loads[0].wait()
+    loads[1].wait()
     cols[...] = jnp.dot(order, up[...], preferred_element_type=F32).astype(BF16)
 
     def fill(n):
@@ -156,7 +161,7 @@
         tells.append(cp)
 
     choose(1)
-    for cp in loads[1:]:
+    for cp in loads[2:]:
         cp.wait()
     packed[...] = lax.dot_general(pick[...], act[...], NT, preferred_element_type=F32).astype(BF16)
     none = jnp.zeros((RANK, FEATURES), BF16)
@@ -164,7 +169,7 @@
     sides += lax.dot_general(packed[512:1024, :], jnp.concatenate([none, pin[...]], 0), NT, preferred_element_type=F32)
     part[...] = sides.reshape(TENSOR, 32, 128)
     halves = []
-    for d in range(1, TENSOR):
+    for d in FAR:
         to = lax.rem(t + d, TENSOR)
         cp = remote(part.at[to], parts.at[t], isend.at[d - 1], irecv.at[d - 1], g, to)
         cp.start()
@@ -246,7 +251,7 @@
             sds((1,), I32),
             sds((8, 128), F32),
         ),
-        in_specs=[smem] * 3 + [vmem] * 3 + [hbm] * 3,
+        in_specs=[smem] * 3 + [hbm] * 6,
         out_specs=(hbm, hbm, hbm, vmem, vmem, smem, vmem),
         scratch_shapes=[
             pltpu.VMEM((TOKENS, TOKENS), BF16),
@@ -260,7 +265,10 @@
             pltpu.VMEM((FEATURES, TOKENS), BF16),
             pltpu.VMEM((FEATURES, TOKENS), BF16),
             pltpu.VMEM((RANK, FEATURES), BF16),
-            dma((3,)),
+            pltpu.VMEM((SEQS, LEN), I32),
+            pltpu.VMEM((SEQS, 16), F32),
+            pltpu.VMEM((SEQS, 16), F32),
+            dma((6,)),
             dma((4,)),
             dma((16,)),
             dma((16,)),
@@ -287,19 +295,6 @@
     total = skip + pairs
     early = skip + PRE
     groups = total // GROUP
-    barrier = greet(g, t)
-    for d in range(GROUPS):
-        for h in range(2):
-            of, at = lax.rem(g + d, GROUPS), 2 * g + h
-
-            def tell(of=of, at=at):
-                pl.semaphore_signal(barrier, inc=1, device_id={"dp": of, "tensor": at}, device_id_type=MESH)
-
-            if d == 0:
-                pl.when(at != t)(tell)
-            else:
-                tell()
-
     wide = MODEL // 4
     first_loads = []
     for par in range(2):
@@ -317,7 +312,22 @@
     for i in range(4):
         at = slice(i * wide, (i + 1) * wide)
         last_loads.append(pltpu.make_async_copy(w_h.at[:, at], w.at[:, at], load.at[10 + i]))
-    for cp in first_loads + factor_loads + last_loads:
+    for cp in first_loads:
+        cp.start()
+    barrier = greet(g, t)
+    for d in range(GROUPS):
+        for h in range(2):
+            of, at = lax.rem(g + d, GROUPS), 2 * g + h
+
+            def tell(of=of, at=at):
+                pl.semaphore_signal(barrier, inc=1, device_id={"dp": of, "tensor": at}, device_id_type=MESH)
+
+            if d == 0:
+                pl.when(at != t)(tell)
+            else:
+                tell()
+
+    for cp in factor_loads + last_loads:
         cp.start()
     mates = TENSOR - 1 + GROUPS - 1 + TENSOR
     pl.semaphore_wait(barrier, mates - jnp.where(column_group == g, 1, 0))
@@ -357,7 +367,6 @@
     def turn(q, parity):
         for i in range(4):
             second(q, i, 0).wait_recv()
-        for i in range(4):
             second(q, i, 1, parity).start()
 
     def arrive(q, parity):
@@ -369,7 +378,7 @@
             ahead(i, 0).start()
     send(skip)
     gathers = []
-    for d in range(1, TENSOR):
+    for d in FAR:
         cp = remote(ins.at[t], ins.at[t], asend.at[d - 1], arecv.at[d - 1], g, lax.rem(t + d, TENSOR))
         cp.start()
         gathers.append(cp)
@@ -413,7 +422,7 @@
                 u[back, c + 256 : c + 384] = pltpu.roll(jnp.where(lanes, right, left), 64, 1).astype(BF16)
 
     def multiply(n, count, i):
-        units = pl.ds(pl.multiple_of(i * 576, 16), 576)
+        units = pl.ds(pl.multiple_of(i * 864, 16), 864)
         acc = None
         for k in range(4):
             at = slice(k * wide, (k + 1) * wide)
@@ -443,13 +452,11 @@
         cp.wait()
     factor(0, GROUP)
 
-    def gather_in(n):
-        for e in range(GROUP):
-            pl.when(n * GROUP + e >= skip)(lambda e=e: arrive(n * GROUP + e, e))
-
-        @pl.loop(0, GROUP)
-        def _(e):
-            pl.when(n * GROUP + e >= skip)(lambda: assemble(n * GROUP + e, e))
+    def take(q, one):
+        @pl.when(q >= skip)
+        def _():
+            arrive(q, one)
+            assemble(q, one)
 
     def pass_on(q, parity):
         pl.when((q >= skip) & (q < total))(lambda: turn(q, parity))
@@ -471,10 +478,11 @@
 
     @pl.loop(0, groups + 1)
     def _(n):
+        pl.when(n >= 1)(lambda: take((n - 1) * GROUP, 0))
         pass_on(n * GROUP, 0)
-        pl.when(n >= 1)(lambda: gather_in(n - 1))
-
-        @pl.loop(0, 3)
+        pl.when(n >= 1)(lambda: take((n - 1) * GROUP + 1, 1))
+
+        @pl.loop(0, 2)
         def _(i):
             pl.when(n >= 1)(lambda: multiply(n - 1, GROUP, i))
 
@@ -502,28 +510,45 @@
     upper = (iota((TENSOR, 8, 128), 2) >= 64) & (iota((TENSOR, 8, 128), 1) >= 4)
     outs[...] = jnp.where(upper, gap[4:5, 0:1].reshape(1, 1, 1), mine)
     reduces = []
-    for d in range(1, TENSOR):
+    for d in FAR:
         to = lax.rem(t + d, TENSOR)
         cp = remote(outs.at[to], sides.at[t], rsend.at[d - 1], rrecv.at[d - 1], g, to)
         cp.start()
         reduces.append(cp)
     sides[t] = outs[t]
+    @pl.loop(skip, total)
+    def _(q):
+        for i in range(4):
+            second(q, i, 0).wait_send()
+
+    for q in range(skip, total):
+        for i in range(4):
+            second(q, i, 1, q % 2).wait_send()
+
+    if pairs > PRE:
+        for hop in range(2):
+            for i in range(4):
+                ahead(i, hop).wait_send()
+    for cp in gathers:
+        cp.wait_send()
     for cp in reduces:
         cp.wait_recv()
     summed = jnp.sum(sides[...], axis=0)
     coeff = -BETA * jax.nn.sigmoid(-BETA * summed[:, 64:65])
-    fin[...] = jnp.where(iota((8, 128), 1) < 64, coeff * summed, 0.0)
+    scaled = coeff * summed
+    even, odd = (jnp.concatenate([scaled[i + e : i + e + 1] for i in (0, 2, 4, 6)], 0) for e in (0, 1))
+    fin[...] = jnp.where(iota((4, 128), 1) < 64, even, pltpu.roll(odd, 64, 1))
 
     ends = []
+    own_column = remote(fin, coled.at[g, column_part], csend.at[0], crecv.at[g, column_part], column_group, t)
+    for d in FAR:
+        ends.append(remote(fin, coled.at[g, column_part], csend.at[d], crecv.at[g, column_part], column_group, lax.rem(t + d, TENSOR)))
+    for d in FAR:
+        ends.append(remote(fin, every.at[t], gsend.at[d - 1], grecv.at[d - 1], g, lax.rem(t + d, TENSOR)))
     for d in range(1, GROUPS):
         ends.append(remote(fin, rowed.at[g], psend.at[d - 1], precv.at[d - 1], lax.rem(g + d, GROUPS), t))
-    for d in range(1, TENSOR):
-        ends.append(remote(fin, coled.at[g, column_part], csend.at[d], crecv.at[g, column_part], column_group, lax.rem(t + d, TENSOR)))
-    for d in range(1, TENSOR):
-        ends.append(remote(fin, every.at[t], gsend.at[d - 1], grecv.at[d - 1], g, lax.rem(t + d, TENSOR)))
     for cp in ends:
         cp.start()
-    own_column = remote(fin, coled.at[g, column_part], csend.at[0], crecv.at[g, column_part], column_group, t)
     pl.when(column_group != g)(own_column.start)
 
     @pl.when(column_group == g)
@@ -532,9 +557,11 @@
 
     rowed[g] = fin[...]
     every[t] = fin[...]
-
-    for d in range(1, GROUPS):
-        ends[d - 1].wait_recv()
+    for cp in reduces:
+        cp.wait_send()
+
+    for cp in ends[-(GROUPS - 1) :]:
+        cp.wait_recv()
     for d in range(GROUPS):
         for h in range(2):
             of = lax.rem(g + d, GROUPS)
@@ -544,29 +571,15 @@
             else:
                 cp.wait_recv()
 
-    for cp in ends[-(TENSOR - 1) :]:
+    for cp in ends[TENSOR - 1 : 2 * TENSOR - 2]:
         cp.wait_recv()
     ends_o[0:8] = rowed[...]
-    ends_o[8:24] = coled[...].reshape(TENSOR, 8, 128)
+    ends_o[8:24] = coled[...].reshape(TENSOR, 4, 128)
     ends_o[24:40] = every[...]
 
     pl.when(column_group != g)(own_column.wait_send)
-    for cp in ends + reduces + gathers:
+    for cp in ends:
         cp.wait_send()
-
-    @pl.loop(skip, total)
-    def _(q):
-        for i in range(4):
-            second(q, i, 0).wait_send()
-
-    for q in range(skip, total):
-        for i in range(4):
-            second(q, i, 1, q % 2).wait_send()
-
-    if pairs > PRE:
-        for hop in range(2):
-            for i in range(4):
-                ahead(i, hop).wait_send()
 
 
 def main(pairs, gap, insum, sign, pout, own, g1, pick, gate, upo, w):
@@ -576,7 +589,7 @@
     dma = pltpu.SemaphoreType.DMA
     return pl.pallas_call(
         functools.partial(main_kernel, pairs),
-        out_shape=jax.ShapeDtypeStruct((40, 8, 128), F32),
+        out_shape=jax.ShapeDtypeStruct((40, 4, 128), F32),
         in_specs=[vmem] + [hbm] * 9,
         out_specs=vmem,
         scratch_shapes=[
@@ -594,10 +607,10 @@
             pltpu.VMEM((RANK, 128), F32),
             pltpu.VMEM((TENSOR, 8, 128), F32),
             pltpu.VMEM((TENSOR, 32, 128), BF16),
-            pltpu.VMEM((8, 128), F32),
-            pltpu.VMEM((TENSOR, 8, 128), F32),
-            pltpu.VMEM((GROUPS, 8, 128), F32),
-            pltpu.VMEM((GROUPS, 2, 8, 128), F32),
+            pltpu.VMEM((4, 128), F32),
+            pltpu.VMEM((TENSOR, 4, 128), F32),
+            pltpu.VMEM((GROUPS, 4, 128), F32),
+            pltpu.VMEM((GROUPS, 2, 4, 128), F32),
             dma((14,)),
             dma((TENSOR - 1,)),
             dma((TENSOR - 1,)),
@@ -621,27 +634,17 @@
 
 
 def final_kernel(ends, grads_o, fisher_o):
-    def joined(at, i):
-        lanes = iota((GROUPS, 128), 1) < 64
-        got = []
-        for p in range(2):
-            one, two = ends[at, p * 4 + i], ends[at, p * 4 + i + 1]
-            got.append(jnp.where(lanes, one, pltpu.roll(two, 64, 1)))
-        return got
-
-    columns = [joined(pl.ds(8 + h, GROUPS, 2), i) for h in range(2) for i in (0, 2)]
-    rows = [joined(slice(0, GROUPS), i) for i in (0, 2)]
-    right = jnp.concatenate([jnp.concatenate(pair, 0) for pair in columns], 1)
-    left = jnp.concatenate([jnp.concatenate(pair, 0) for pair in rows], 1)
+    def joined(at, h):
+        return jnp.concatenate([ends[at, h], ends[at, 2 + h]], 0)
+
+    right = jnp.concatenate([joined(pl.ds(8 + part, GROUPS, 2), h) for part in range(2) for h in range(2)], 1)
+    left = jnp.concatenate([joined(slice(0, GROUPS), h) for h in range(2)], 1)
     fisher_o[...] = lax.dot_general(left, right, TN, precision=lax.Precision.HIGHEST, preferred_element_type=F32)
-    lanes = iota((2, 128), 1) < 64
     for c in range(TENSOR):
         tile = ends[24 + c]
-        for i in (0, 2):
-            one = jnp.concatenate([tile[i : i + 1], tile[4 + i : 5 + i]], 0)
-            two = jnp.concatenate([tile[i + 1 : i + 2], tile[5 + i : 6 + i]], 0)
-            at = c * 256 + i * 64
-            grads_o[:, at : at + 128] = jnp.where(lanes, one, pltpu.roll(two, 64, 1))
+        for h in range(2):
+            at = c * 256 + h * 128
+            grads_o[:, at : at + 128] = jnp.concatenate([tile[h : h + 1], tile[2 + h : 3 + h]], 0)
 
 
 def final(ends):

time: 83.2 us -> 81.9 us (0.984)
  Pallas kernels: 81.1 us -> 79.9 us
    pallas_call x1, Pallas kernels: 21.2 us -> 20.1 us  [stage(): pl.pallas_call(stage_kernel, out_shape=(sds((2, ALL_PAIRS, ROWS, 128), BF...]
where the time goes in v4:
time: 81.9 us; the launch traced here: 81.7 us
  Pallas kernels  79.9 us (98%)
  between operations  1.29 us (2%)
    pallas_call x1, Pallas kernels, main(): pl.pallas_call(functools.partial(main_kernel, pairs), out_shape=jax.Shape...  58.4 us
    pallas_call x1, Pallas kernels, stage(): pl.pallas_call(stage_kernel, out_shape=(sds((2, ALL_PAIRS, ROWS, 128), BF...  20.1 us

profile of v4, /device:TPU:1, one launch (start us, length us, event | category | flops | bytes accessed | tf_op | source)
XLA Modules:
  0.0 81.7 jit_solution(4484474835598814084)
XLA Ops:
  0.6 0.0 copy-start
  0.6 0.0 copy-start.1
  0.7 20.1 %stage.1 = (bf16[2,8,160,128]{3,2,1,0:T(8,128)(2,1)}, bf16[2,4,4,160,128]{4,3,2,1,0:T(8,128)(2,1)}, bf16[1024,1024]{1,0:T(8,128)(2,1)}, bf16[1024,128]{1,0:T(8,1...) custom-call(s32[1,4]{1,0:T(1,128)} %perm.1, s32[2]{0:T(128)} %first.1, s32[4]{0:T(128)} %resp.1, ...), custom_call_target="tpu_custom_call" | custom-call | flops 2000000000 | bytes 8000000 | tf_op jit(solution)/shard_map/stage/pallas_call | solution.py:243
  21.3 0.0 copy-done
  21.4 0.0 copy-done.1
  21.4 58.9 %conditional.1 = (f32[40,4,128]{2,1,0:T(4,128)S(1)}) conditional(s32[]{:T(128)} %bitcast.2, (f32[8,128]{1,0:T(8,128)S(1)}, bf16[32,128]{1,0:T(8,128)(2,1)S(1)}, bf16[1024,128]{1,0:T(8,128)(2,1)S(1)}, bf16[64,1728]{1,0:T(8,128)(2,1)S(1)}, bf16[2,8,160,128]{3,2,1,0:T(8,128)(2,1)}, ...), branch_computations={%region_0.0_spmd, %region_1.0_spmd, %region_2.0_spmd, %region_3.0_... | conditional | flops 25600000000 | bytes 30000008 | solution.py:672
  21.4 58.4 %gather_5.1 = f32[40,4,128]{2,1,0:T(4,128)S(1)} custom-call(f32[8,128]{1,0:T(8,128)S(1)} %get-tuple-element.116.gap, bf16[32,128]{1,0:T(8,128)(2,1)S(1)} %get-tuple-element.117.insum_h, bf16[1024,128]{1,0:T(8,128)(2,1)S(1)} %get-tuple-element.118.sign_h, bf16[64,1728]{1,0:T(8,128)(2,1)S(1)} %get-tuple-element.119.pout_h, ...), custom_call_target="tpu_custom_call" | custom-call | flops 16000000000 | bytes 30000000 | tf_op jit(solution)/shard_map/cond/branch_1_fun/gather_5/pallas_call | solution.py:590
  80.3 1.4 %final.1 = (f32[2,4096]{1,0:T(2,128)}, f32[256,512]{1,0:T(8,128)}) custom-call(f32[40,4,128]{2,1,0:T(4,128)S(1)} %get-tuple-element.172.ends), custom_call_target="tpu_custom_call" | custom-call | flops 4000000 | bytes 700000 | tf_op jit(solution)/shard_map/final/pallas_call | solution.py:653
Async XLA Ops:
  0.6 20.7 %copy-start = (bf16[1024,1728]{0,1:T(8,128)(2,1)S(1)}, bf16[1024,1728]{0,1:T(8,128)(2,1)}, u32[]{:S(2)}) copy-start(bf16[1024,1728]{0,1:T(8,128)(2,1)} %param.20) | copy-start | bytes 10616836
  0.6 20.7 %copy-start.1 = (bf16[64,1728]{1,0:T(8,128)(2,1)S(1)}, bf16[64,1728]{1,0:T(8,128)(2,1)}, u32[]{:S(2)}) copy-start(bf16[64,1728]{1,0:T(8,128)(2,1)} %param.24) | copy-start | bytes 663556
